TPU v7x, 32 devices: a whole 2x2x4 slice. The times are simulated.
32 devices in a mesh: dp: 8 (over y, x, core), tensor: 4 (over z).
Axes of the slice: x: 2, y: 2, z: 4, core: 2. Of those that a mesh axis runs over, the one named last changes fastest.
Arguments:
- residual_in: bfloat16 [4096, 1024], P(('dp', 'tensor')), may hold values from -6 to 6
- norm1_gain: float32 [1024], replicated, may hold values from 0.25 to 1.75
- w_query: bfloat16 [1024, 1024], P('dp', 'tensor'), may hold values from -0.1875 to 0.1875
- key_weight: bfloat16 [1024, 512], P('dp', 'tensor'), may hold values from -0.1875 to 0.1875
- value_weight: bfloat16 [1024, 512], P('dp', 'tensor'), may hold values from -0.1875 to 0.1875
- w_out: bfloat16 [1024, 1024], P('dp', 'tensor'), may hold values from -0.5 to 0.5
- norm2_gain: float32 [1024], replicated, may hold values from 0.25 to 1.75
- w_gate: bfloat16 [16, 1024, 512], P(None, 'dp', 'tensor'), may hold values from -0.1875 to 0.1875
- w_up: bfloat16 [16, 1024, 512], P(None, 'dp', 'tensor'), may hold values from -0.1875 to 0.1875
- w_down: bfloat16 [16, 1024, 512], P(None, 'dp', 'tensor'), may hold values from -0.75 to 0.75
- expert_ids: int32 [4096, 8], P('dp'), may hold values from 0 to 15, all different within a row; in each aligned block of 512 rows (0 to 511, 512 to 1023, ...) at most 288 rows name the same one
- gate_weights: float32 [4096, 8], P('dp'), may hold values from 0.06 to 0.25
- out_grad: bfloat16 [4096, 1024], P(('dp', 'tensor')), may hold values from -6 to 6
Outputs:
- residual_out: bfloat16 [4096, 1024], P(('dp', 'tensor'))
- input_grad: float32 [4096, 1024], P(('dp', 'tensor'))
- norm1_gain_grad: float32 [1024], replicated
- w_query_grad: float32 [1024, 1024], P('dp', 'tensor')
- w_key_grad: float32 [1024, 512], P('dp', 'tensor')
- w_value_grad: float32 [1024, 512], P('dp', 'tensor')
- w_out_grad: float32 [1024, 1024], P('dp', 'tensor')
- norm2_gain_grad: float32 [1024], replicated
- w_gate_grad: float32 [16, 1024, 512], P(None, 'dp', 'tensor')
- w_up_grad: float32 [16, 1024, 512], P(None, 'dp', 'tensor')
- w_down_grad: float32 [16, 1024, 512], P(None, 'dp', 'tensor')
Inputs may be any that keep to these rules, and one draw needn't show every extreme that they name: `expert_ids`: each row names 8 different experts. Among the 512 rows of one index of dp no expert is named by more than 288 rows.
All inputs are finite; a program needn't handle non-finite values.
Results may differ from a plain program's by a relative error of at most 0.013.
Values may be sent and summed in bfloat16 or wider, within the bound.
A program may use at most 192 MiB of HBM per device.

v0:
```python
import functools

import jax
import jax.numpy as jnp
from jax import lax
from jax.experimental import pallas as pl
from jax.experimental.pallas import tpu as pltpu
from jax.sharding import PartitionSpec as P

MODEL_WIDTH = 1024
HEAD_SIZE = 64
TOP = 8
LEN = 512
CAP = 288


EPS = 1e-06
THETA = 10000.0


def rope_tables(length, head_width):
    frequency = THETA ** (-(2.0 * jnp.arange(head_width // 2, dtype=jnp.float32)) / head_width)
    angles = jnp.arange(length, dtype=jnp.float32)[:, None] * frequency[None, :]
    return (jnp.cos(angles), jnp.sin(angles))


def apply_rotary(vector, cosine_table, sine_table):
    middle = vector.shape[-1] // 2
    leading = vector[..., :middle]
    trailing = vector[..., middle:]
    return jnp.concatenate(
        [
            leading * cosine_table - trailing * sine_table,
            trailing * cosine_table + leading * sine_table,
        ],
        axis=-1,
    )


def rotate_back(vector, cosine_table, sine_table):
    middle = vector.shape[-1] // 2
    leading = vector[..., :middle]
    trailing = vector[..., middle:]
    return jnp.concatenate(
        [
            leading * cosine_table + trailing * sine_table,
            trailing * cosine_table - leading * sine_table,
        ],
        axis=-1,
    )


def rms_factor(vector):
    return lax.rsqrt(jnp.mean(vector * vector, axis=-1, keepdims=True) + EPS)


def norm_back(vector, factor, gain_vec, grad_in):
    tilted = grad_in * gain_vec
    gain_part = jnp.sum(grad_in * vector * factor, axis=0)
    cubed = factor * factor * factor
    back = factor * tilted - vector * cubed * jnp.mean(tilted * vector, axis=-1, keepdims=True)
    return (back, gain_part)


BF = jnp.bfloat16
F32 = jnp.float32
REL = (0, 2, 4, 6, 1, 3, 5, 7)


def swap(value, axis, bit):
    size = lax.axis_size(axis)
    return lax.ppermute(value, axis, [(i, i ^ bit) for i in range(size)])


def mm(left, right):
    return jnp.dot(left, right, preferred_element_type=F32)


def mm_t(left, right):
    return lax.dot_general(left, right, (((1,), (1,)), ((), ())), preferred_element_type=F32)


def t_mm(left, right):
    return lax.dot_general(left, right, (((0,), (0,)), ((), ())), preferred_element_type=F32)


def reorder_kernel(inverse, *refs):
    count = len(refs) // 2
    me = lax.axis_index("dp")
    for p in range(8):
        if inverse:
            s = jnp.bitwise_xor(me, p)
            block = (s % 2) * 4 + ((s // 4) % 2) * 2 + (s // 2) % 2
        else:
            block = jnp.bitwise_xor(me, REL[p])
        start = pl.multiple_of(block * 128, 128)
        for taken, given in zip(refs[:count], refs[count:]):
            given[:, p * 128 : (p + 1) * 128] = taken[:, pl.ds(start, 128)]


def reorder(values, inverse):
    if lax.axis_size("dp") != 8:
        return values
    return pl.pallas_call(
        functools.partial(reorder_kernel, inverse),
        out_shape=[jax.ShapeDtypeStruct(v.shape, v.dtype) for v in values],
        in_specs=[pl.BlockSpec(memory_space=pltpu.VMEM)] * len(values),
        out_specs=[pl.BlockSpec(memory_space=pltpu.VMEM)] * len(values),
    )(*values)


def experts_kernel(
    way, x, dy, spread, pair, second, pair_o, second_o, n2, mixed, hg, gg, ug, wg, wu, wd
):
    pieces = (pair, second, pair_o, second_o)
    for core in range(2):
        for late in range(2):
            for j in range(2):
                place = core * 4 + (late * 2 + j if way == 0 else j * 2 + late)
                rows = slice(place * 128, (place + 1) * 128)
                for k, weight in enumerate((wg, wu, wd)):
                    for e in range(2):
                        weight[rows, e * 128 : (e + 1) * 128] = pieces[core * 2 + late][j, k, e]
    gate_proj = mm(x[...], wg[...])
    up_proj = mm(x[...], wu[...])
    hidden_grad = mm(dy[...], wd[...]) * spread[...]
    sigmoid_g = 1.0 / (1.0 + jnp.exp(-gate_proj))
    activated = gate_proj * sigmoid_g
    hidden = (activated * up_proj * spread[...]).astype(BF)
    gate_grad = (
        hidden_grad * up_proj * sigmoid_g * (1.0 + gate_proj * (1.0 - sigmoid_g))
    ).astype(BF)
    up_grad = (hidden_grad * activated).astype(BF)
    hg[...] = hidden
    gg[...] = gate_grad
    ug[...] = up_grad
    n2_step = mm_t(gate_grad, wg[...]) + mm_t(up_grad, wu[...])
    mixed_step = mm_t(hidden, wd[...])

    @pl.when(pl.program_id(0) == 0)
    def _():
        n2[...] = n2_step
        mixed[...] = mixed_step

    @pl.when(pl.program_id(0) != 0)
    def _():
        n2[...] += n2_step
        mixed[...] += mixed_step


def experts_part(way, x, dy, spread, pieces):
    rows, width = x.shape
    half = pieces[0].shape[2]
    whole = pl.BlockSpec((rows, width), lambda i: (0, 0))
    tile = pl.BlockSpec((rows, 256), lambda i: (0, i))
    piece = pl.BlockSpec((2, 3, 2, 128, 128), lambda i: (0, 0, i, 0, 0))
    hidden_shape = jax.ShapeDtypeStruct((rows, half * 128), BF)
    return pl.pallas_call(
        functools.partial(experts_kernel, way),
        grid=(half // 2,),
        in_specs=[whole, whole, tile, piece, piece, piece, piece],
        out_specs=[whole, whole, tile, tile, tile],
        out_shape=[jax.ShapeDtypeStruct((rows, width), F32)] * 2 + [hidden_shape] * 3,
        scratch_shapes=[pltpu.VMEM((width, 256), BF)] * 3,
        compiler_params=pltpu.CompilerParams(vmem_limit_bytes=50 * 2**20),
        cost_estimate=pl.CostEstimate(
            flops=12 * rows * width * half * 128, bytes_accessed=16 * 2**20, transcendentals=0
        ),
    )(x, dy, spread, *pieces)


def weight_grads_kernel(way, x_t, dy_t, hg, gg, ug, sent, kept):
    for k, (left, right) in enumerate(((x_t, gg), (x_t, ug), (dy_t, hg))):
        grad = mm(left[...], right[...]).astype(BF)
        for core in range(2):
            for y in range(2):
                for x in range(2):
                    place = core * 4 + y * 2 + x
                    slot = (1 - x) * 2 + 1 - y if way == 0 else (1 - y) * 2 + 1 - x
                    for e in range(2):
                        (sent if core else kept)[slot, k, e] = grad[
                            place * 128 : (place + 1) * 128, e * 128 : (e + 1) * 128
                        ]


def weight_grads(way, x_t, dy_t, hg, gg, ug):
    width, rows = x_t.shape
    half = hg.shape[1] // 128
    whole = pl.BlockSpec((width, rows), lambda i: (0, 0))
    tile = pl.BlockSpec((rows, 256), lambda i: (0, i))
    quad = pl.BlockSpec((4, 3, 2, 128, 128), lambda i: (0, 0, i, 0, 0))
    return pl.pallas_call(
        functools.partial(weight_grads_kernel, way),
        grid=(half // 2,),
        in_specs=[whole, whole, tile, tile, tile],
        out_specs=[quad, quad],
        out_shape=[jax.ShapeDtypeStruct((4, 3, half, 128, 128), BF)] * 2,
        compiler_params=pltpu.CompilerParams(vmem_limit_bytes=50 * 2**20),
        cost_estimate=pl.CostEstimate(
            flops=6 * rows * width * half * 128, bytes_accessed=10 * 2**20, transcendentals=0
        ),
    )(x_t, dy_t, hg, gg, ug)


WAYS = ((2, 4), (4, 2))


def sum_pieces(way, sent, kept):
    near, far = WAYS[way]
    core = swap(sent, "dp", 1)
    first = swap(add_low(kept[:2], core[:2]), "dp", near)
    held = kept[2:].astype(F32) + core[2:].astype(F32) + first.astype(F32)
    return held[1] + swap(held[0].astype(BF), "dp", far).astype(F32)


def gather_rows(shards):
    ways = [(2, 4) if i % 2 == 0 else (4, 2) for i in range(len(shards))]
    if lax.axis_size("dp") != 8:
        return [lax.all_gather(s, "dp", axis=0, tiled=True) for s in shards]
    first = [swap(s, "dp", w[0]) for s, w in zip(shards, ways)]
    pairs = [jnp.stack([s, f]) for s, f in zip(shards, first)]
    second = [swap(p, "dp", w[1]) for p, w in zip(pairs, ways)]
    quads = [
        jnp.stack([p, s], axis=0 if w[1] == 4 else 1) for p, s, w in zip(pairs, second, ways)
    ]
    third = [swap(q, "dp", 1) for q in quads]
    return [
        jnp.concatenate([q, t]).reshape(-1, q.shape[-1]) for q, t in zip(quads, third)
    ]


def add_low(a, b):
    return (a.astype(F32) + b.astype(F32)).astype(BF)


def scatter_rows(full, way):
    if lax.axis_size("dp") != 8:
        return lax.psum_scatter(full, "dp", scatter_dimension=0, tiled=True).astype(F32)
    columns = full.shape[1]
    quads = full.reshape(2, 2, 2, 128, columns)
    other = swap(quads[1], "dp", 1)
    held = add_low(quads[0], other)
    if way == 0:
        pair = add_low(held[:, 0], swap(held[:, 1], "dp", 2))
        last = swap(pair[1], "dp", 4)
    else:
        pair = add_low(held[0], swap(held[1], "dp", 4))
        last = swap(pair[1], "dp", 2)
    return pair[0].astype(F32) + last.astype(F32)


def total(value):
    for axis in ("dp", "tensor"):
        bit = 1
        while bit < lax.axis_size(axis):
            value = value + swap(value, axis, bit)
            bit *= 2
    return value


def gather_tokens(rows):
    me = lax.axis_index("tensor")
    size = lax.axis_size("tensor")
    held = jnp.stack([rows] + [swap(rows, "tensor", r) for r in range(1, size)])
    return jnp.concatenate(
        [lax.dynamic_index_in_dim(held, me ^ b, 0, keepdims=False) for b in range(size)]
    )


def scatter_tokens(full):
    me = lax.axis_index("tensor")
    size = lax.axis_size("tensor")
    blocks = full.reshape(size, -1, full.shape[-1])
    out = lax.dynamic_index_in_dim(blocks, me, 0, keepdims=False).astype(F32)
    for r in range(1, size):
        piece = lax.dynamic_index_in_dim(blocks, me ^ r, 0, keepdims=False)
        out = out + swap(piece, "tensor", r).astype(F32)
    return out


def rows_first(weight):
    return jnp.swapaxes(weight, 0, 1).reshape(weight.shape[1], -1)


def experts_first(grad, experts):
    return jnp.swapaxes(grad.reshape(grad.shape[0], experts, -1), 0, 1)


def local(
    residual_in,
    norm1_gain,
    w_query,
    key_weight,
    value_weight,
    w_out,
    norm2_gain,
    w_gate,
    w_up,
    w_down,
    expert_ids,
    gate_weights,
    out_grad,
):
    group_rows = expert_ids.shape[0]
    sequences = group_rows // LEN
    heads_q = w_query.shape[1] // HEAD_SIZE
    heads_kv = key_weight.shape[1] // HEAD_SIZE
    per_kv = heads_q // heads_kv
    experts = w_gate.shape[0]
    factor_s = HEAD_SIZE ** (-0.5)
    bf_type = jnp.bfloat16
    f_type = jnp.float32
    relative = lax.axis_size("dp") == 8
    q_width, k_width = w_query.shape[1], key_weight.shape[1]
    residual, cotangent, gain_one, gain_two = reorder(
        (residual_in, out_grad, norm1_gain[None, :], norm2_gain[None, :]), False
    )
    residual = residual.astype(f_type)
    gain_one, gain_two = gain_one[0], gain_two[0]
    full_qk, full_vo = gather_rows(
        [
            jnp.concatenate([w_query, key_weight], axis=1),
            jnp.concatenate([value_weight, w_out], axis=1),
        ]
    )
    full_v, full_o = full_vo[:, :k_width], full_vo[:, k_width:]
    factor_one = rms_factor(residual)
    normed = lax.all_gather(
        (residual * factor_one * gain_one).astype(bf_type), "tensor", axis=0, tiled=True
    )
    half = experts // 2
    parts = (slice(0, half), slice(half, None))
    if relative:
        shards = [jnp.stack([w_gate[p], w_up[p], w_down[p]]) for p in parts]
        shards, full_qk = lax.optimization_barrier((shards, full_qk))
        firsts = [swap(w, "dp", way[0]) for w, way in zip(shards, WAYS)]
        pairs = [jnp.stack([w, f]) for w, f in zip(shards, firsts)]
        seconds = [swap(p, "dp", way[1]) for p, way in zip(pairs, WAYS)]
    else:
        shards = [
            jnp.concatenate([rows_first(w_gate[p]), rows_first(w_up[p])], axis=1) for p in parts
        ] + [rows_first(w_down[p]) for p in parts]
        shards, full_qk = lax.optimization_barrier((shards, full_qk))
        gu_a, gu_b, d_a, d_b = gather_rows(shards)
    grad_rows = gather_tokens(cotangent)
    cosine_table, sine_table = rope_tables(LEN, HEAD_SIZE)
    cosine_table = cosine_table[:, None, :]
    sine_table = sine_table[:, None, :]
    qk_raw = mm(normed, full_qk)
    query_raw = qk_raw[:, :q_width].reshape(sequences, LEN, heads_q, HEAD_SIZE)
    query = apply_rotary(query_raw, cosine_table, sine_table).astype(bf_type)
    keys_raw = qk_raw[:, q_width:].reshape(sequences, LEN, heads_kv, HEAD_SIZE)
    key_rows = apply_rotary(keys_raw, cosine_table, sine_table).astype(bf_type)
    value_rows = mm(normed, full_v).astype(bf_type).reshape(sequences, LEN, heads_kv, HEAD_SIZE)
    causal = jnp.arange(LEN)[:, None] >= jnp.arange(LEN)[None, :]

    def score_block(query_seq, key_seq):
        grouped = query_seq.reshape(LEN, heads_kv, per_kv, HEAD_SIZE)
        scores = (
            jnp.einsum("qkgd,skd->kgqs", grouped, key_seq, preferred_element_type=f_type) * factor_s
        )
        return jnp.where(causal, scores, -1e30)

    def forward_one(pieces):
        query_seq, key_seq, value_seq = pieces
        scores = score_block(query_seq, key_seq)
        row_max = jnp.max(scores, axis=-1, keepdims=True)
        exp_scores = jnp.exp(scores - row_max)
        row_sum = jnp.sum(exp_scores, axis=-1, keepdims=True)
        chances = (exp_scores / row_sum).astype(bf_type)
        attended = jnp.einsum("kgqs,skd->qkgd", chances, value_seq, preferred_element_type=f_type)
        return (attended.reshape(LEN, heads_q * HEAD_SIZE), (row_max + jnp.log(row_sum))[..., 0])

    attended, log_sums = lax.map(forward_one, (query, key_rows, value_rows))
    heads_out = attended.reshape(group_rows, heads_q * HEAD_SIZE).astype(bf_type)
    middle = residual + lax.psum_scatter(
        mm_t(heads_out, full_o).astype(bf_type), "tensor", scatter_dimension=0, tiled=True
    ).astype(f_type)
    factor_two = rms_factor(middle)
    normed_two_rows = (middle * factor_two * gain_two).astype(bf_type)
    normed_two = lax.all_gather(normed_two_rows, "tensor", axis=0, tiled=True)
    chosen = expert_ids[:, :, None] == jnp.arange(experts, dtype=jnp.int32)[None, None, :]
    mixing = jnp.sum(jnp.where(chosen, gate_weights[:, :, None], 0.0), axis=1)
    if relative:
        pairs, seconds, _ = lax.optimization_barrier((pairs, seconds, normed_two_rows))
        spread = jnp.broadcast_to(
            mixing[:, :, None], (group_rows, experts, 128)
        ).reshape(group_rows, experts * 128)
        results = []
        for way in range(2):
            pieces = (pairs[way], seconds[way], swap(pairs[way], "dp", 1))
            pieces = pieces + (swap(seconds[way], "dp", 1),)
            columns = spread[:, way * half * 128 : (way + 1) * half * 128]
            results.append(experts_part(way, normed_two, grad_rows, columns, pieces))
        normed_two_part = results[0][0] + results[1][0]
        mixed_part = results[0][1] + results[1][1]
    else:
        mixed_part, normed_two_part, low_grads = 0.0, 0.0, []
        for mix, gu, down in ((mixing[:, :half], gu_a, d_a), (mixing[:, half:], gu_b, d_b)):
            width = down.shape[1]
            spread = jnp.broadcast_to(
                mix[:, :, None], (group_rows, half, width // half)
            ).reshape(group_rows, width)
            both = mm(normed_two, gu)
            gate_proj, up_proj = both[:, :width], both[:, width:]
            sigmoid_g = jax.nn.sigmoid(gate_proj)
            activated = gate_proj * sigmoid_g
            hidden = (activated * up_proj * spread).astype(bf_type)
            hidden_grad = mm(grad_rows, down) * spread
            gate_grad = hidden_grad * up_proj * sigmoid_g * (1.0 + gate_proj * (1.0 - sigmoid_g))
            up_grad = hidden_grad * activated
            both_grad = jnp.concatenate([gate_grad.astype(bf_type), up_grad.astype(bf_type)], axis=1)
            normed_two_part = normed_two_part + mm_t(both_grad, gu)
            mixed_part = mixed_part + mm_t(hidden, down)
            low_grads.append((both_grad, hidden))
    normed_two_grad = lax.psum_scatter(
        normed_two_part.astype(bf_type), "tensor", scatter_dimension=0, tiled=True
    ).astype(f_type)
    residual_out = (middle + scatter_tokens(mixed_part.astype(bf_type))).astype(bf_type)
    if relative:
        x_t, dy_t = normed_two.T, grad_rows.T
        sums = []
        for way in range(2):
            sent, kept = weight_grads(way, x_t, dy_t, *results[way][2:])
            sums.append(sum_pieces(way, sent, kept))
        w_gate_grad, w_up_grad, w_down_grad = (
            jnp.concatenate([sums[0][k], sums[1][k]]) for k in range(3)
        )
    else:
        gu_grads, down_grads = [], []
        for way, (both_grad, hidden) in enumerate(low_grads):
            gu_grads.append(scatter_rows(t_mm(normed_two, both_grad).astype(bf_type), way))
            down_grads.append(scatter_rows(t_mm(grad_rows, hidden).astype(bf_type), way))
        width = down_grads[0].shape[1]
        w_gate_grad = jnp.concatenate([experts_first(g[:, :width], half) for g in gu_grads])
        w_up_grad = jnp.concatenate([experts_first(g[:, width:], half) for g in gu_grads])
        w_down_grad = jnp.concatenate([experts_first(g, half) for g in down_grads])
    back_two, gain_two_part = norm_back(middle, factor_two, gain_two, normed_two_grad)
    middle_grad = cotangent.astype(f_type) + back_two
    middle_rows = lax.all_gather(middle_grad.astype(bf_type), "tensor", axis=0, tiled=True)
    grad_out_w = t_mm(middle_rows, heads_out)
    heads_grad = jnp.dot(middle_rows, full_o, preferred_element_type=f_type).astype(bf_type)
    heads_grad = heads_grad.reshape(sequences, LEN, heads_q * HEAD_SIZE)

    def backward_one(pieces):
        query_seq, key_seq, value_seq, log_seq, grad_seq = pieces
        scores = score_block(query_seq, key_seq)
        chances = jnp.exp(scores - log_seq[..., None])
        grad_grouped = grad_seq.reshape(LEN, heads_kv, per_kv, HEAD_SIZE)
        grad_value = jnp.einsum(
            "kgqs,qkgd->skd", chances.astype(bf_type), grad_grouped, preferred_element_type=f_type
        )
        grad_chances = jnp.einsum(
            "qkgd,skd->kgqs", grad_grouped, value_seq, preferred_element_type=f_type
        )
        grad_scores = (
            chances * (grad_chances - jnp.sum(grad_chances * chances, axis=-1, keepdims=True))
        ).astype(bf_type)
        grad_query = (
            jnp.einsum("kgqs,skd->qkgd", grad_scores, key_seq, preferred_element_type=f_type)
            * factor_s
        )
        grouped = query_seq.reshape(LEN, heads_kv, per_kv, HEAD_SIZE)
        grad_key = (
            jnp.einsum("kgqs,qkgd->skd", grad_scores, grouped, preferred_element_type=f_type)
            * factor_s
        )
        return (grad_query.reshape(LEN, heads_q, HEAD_SIZE), grad_key, grad_value)

    query_rgrad, keys_rgrad, values_rgrad = lax.map(
        backward_one, (query, key_rows, value_rows, log_sums, heads_grad)
    )
    query_grad = (
        rotate_back(query_rgrad, cosine_table, sine_table)
        .astype(bf_type)
        .reshape(group_rows, heads_q * HEAD_SIZE)
    )
    keys_grad = (
        rotate_back(keys_rgrad, cosine_table, sine_table)
        .astype(bf_type)
        .reshape(group_rows, heads_kv * HEAD_SIZE)
    )
    values_grad = values_rgrad.astype(bf_type).reshape(group_rows, heads_kv * HEAD_SIZE)
    qk_grad = jnp.concatenate([query_grad, keys_grad], axis=1)
    grad_qk_w = scatter_rows(t_mm(normed, qk_grad).astype(bf_type), 0)
    grad_vo_w = scatter_rows(
        jnp.concatenate([t_mm(normed, values_grad), grad_out_w], axis=1).astype(bf_type), 1
    )
    w_query_grad, w_key_grad = grad_qk_w[:, :q_width], grad_qk_w[:, q_width:]
    w_value_grad, w_out_grad = grad_vo_w[:, :k_width], grad_vo_w[:, k_width:]
    normed_part = mm_t(qk_grad, full_qk) + mm_t(values_grad, full_v)
    gain_one_part = jnp.sum(normed_part * normed.astype(f_type), axis=0) / gain_one
    normed_grad = lax.psum_scatter(
        normed_part.astype(bf_type), "tensor", scatter_dimension=0, tiled=True
    ).astype(f_type)
    back_one, _ = norm_back(residual, factor_one, gain_one, normed_grad)
    gains = jnp.stack([gain_one_part, gain_two_part])
    residual_out, input_grad, gains = reorder(
        (residual_out, middle_grad + back_one, gains), True
    )
    gains = total(gains)
    norm1_gain_grad, norm2_gain_grad = gains[0], gains[1]
    return (
        residual_out,
        input_grad,
        norm1_gain_grad,
        w_query_grad,
        w_key_grad,
        w_value_grad,
        w_out_grad,
        norm2_gain_grad,
        w_gate_grad,
        w_up_grad,
        w_down_grad,
    )


def solution(mesh):
    placed = (
        P(("dp", "tensor"), None),
        P(),
        P("dp", "tensor"),
        P("dp", "tensor"),
        P("dp", "tensor"),
        P("dp", "tensor"),
        P(),
        P(None, "dp", "tensor"),
        P(None, "dp", "tensor"),
        P(None, "dp", "tensor"),
        P("dp", None),
        P("dp", None),
        P(("dp", "tensor"), None),
    )
    return jax.shard_map(
        local,
        mesh=mesh,
        in_specs=placed,
        out_specs=(
            P(("dp", "tensor"), None),
            P(("dp", "tensor"), None),
            P(),
            P("dp", "tensor"),
            P("dp", "tensor"),
            P("dp", "tensor"),
            P("dp", "tensor"),
            P(),
            P(None, "dp", "tensor"),
            P(None, "dp", "tensor"),
            P(None, "dp", "tensor"),
        ),
        check_vma=False,
    )
```

profile of v0, /device:TPU:0, one launch (start us, length us, event | category | flops | bytes accessed | tf_op | source)
XLA Modules:
  0.0 361.1 jit_solution(4085227501889408194)
XLA Ops:
  9.0 3.0 collective-permute-start.3
  12.0 2.0 shard_map.212
  15.9 1.6 fusion.32
  17.6 1.6 collective-permute-start
  20.1 2.9 collective-permute-done
  23.9 2.5 collective-permute-done.4
  26.6 2.2 collective-permute-done.1
  30.8 17.4 %all-gather.4.cloned.1.call-done = bf16[512,1024]{0,1:T(8,128)(2,1)} async-done(((bf16[128,1024]{0,1:T(8,128)(2,1)}), bf16[512,1024]{0,1:T(8,128)(2,1)}) %all-gather.4.cloned.1.call-update) | async-done | bytes 1048592 | tf_op jit(solution)/shard_map/all_gather | solution.py:328
  48.2 1.8 fusion.67
  52.5 1.4 copy-done.11
  55.9 1.5 convolution_convert_fusion
  57.9 1.5 collective-permute-start.10
  59.4 16.3 %collective-permute-done.9 = bf16[3,8,128,128]{3,2,1,0:T(8,128)(2,1)S(1)} collective-permute-done((bf16[3,8,128,128]{3,2,1,0:T(8,128)(2,1)S(1)}, bf16[3,8,128,128]{3,2,1,0:T(8,128)(2,1)S(1)}, u32[]{:S(2)}, u32[]{:S(2)}) %collective-permute-start.9) | collective-permute-done | bytes 786464 | tf_op jit(solution)/shard_map/ppermute | solution.py:72
  77.0 1.8 collective-permute-start.11
  80.1 1.5 collective-permute-start.12
  81.5 1.4 reduce-scatter.10.cloned.1.call-done
  85.9 27.0 %collective-permute-done.11.second = bf16[2,3,8,128,128]{4,3,2,1,0:T(8,128)(2,1)} collective-permute-done((bf16[2,3,8,128,128]{4,3,2,1,0:T(8,128)(2,1)}, bf16[2,3,8,128,128]{4,3,2,1,0:T(8,128)(2,1)}, u32[]{:S(2)}, u32[]{:S(2)}) %collective-permute-start.11) | collective-permute-done | bytes 1572896 | tf_op jit(solution)/shard_map/ppermute | solution.py:72
  113.0 2.8 collective-permute-done.12.second
  116.3 1.9 collective-permute-start.7
  118.1 10.6 %collective-permute-done.6 = bf16[128,1024]{1,0:T(8,128)(2,1)S(1)} collective-permute-done((bf16[128,1024]{1,0:T(8,128)(2,1)S(1)}, bf16[128,1024]{1,0:T(8,128)(2,1)S(1)}, u32[]{:S(2)}, u32[]{:S(2)}) %collective-permute-start.6) | collective-permute-done | bytes 262176 | tf_op jit(solution)/shard_map/ppermute | solution.py:72
  130.1 4.0 %copy.168 = f32[64,8,16,128]{3,1,2,0:T(8,128)} copy(f32[64,8,16,128]{3,2,1,0:T(8,128)S(1)} %bitcast.201) | data formatting | bytes 8388608
  134.1 2.4 collective-permute-start.8
  136.5 4.9 %fusion.63 = (f32[512,1024]{1,0:T(8,128)}, f32[512,1024]{1,0:T(8,128)}) fusion(f32[512,2048]{1,0:T(8,128)} %bitcast.200), kind=kLoop, calls=%fused_computation.178 | loop fusion | bytes 8388608 | tf_op jit(solution)/shard_map/slice | solution.py:393
  141.4 3.3 collective-permute-done.8
  147.4 1.3 copy.124.dy
  148.7 2.3 copy.123.x
  151.0 16.4 %shard_map.213 = (f32[512,1024]{1,0:T(8,128)}, f32[512,1024]{1,0:T(8,128)}, bf16[512,1024]{1,0:T(8,128)(2,1)S(1)}, bf16[512,1024]{1,0:T(8,128)(2,1)S(1)}, bf16[512,1024]{1,0:T(8,128)(2,1)S(1)}) custom-call(bf16[512,1024]{1,0:T(8,128)(2,1)} %copy.123.x, bf16[512,1024]{1,0:T(8,128)(2,1)} %copy.124.dy, f32[512,1024]{1,0:T(8,128)} %get-tuple-element.121.spread, ...), custom_call_target="tpu_custom_call" | custom-call | flops 6442450944 | bytes 16777216 | tf_op jit(solution)/shard_map/pallas_call | solution.py:158
  168.4 16.8 %shard_map.214 = (f32[512,1024]{1,0:T(8,128)}, f32[512,1024]{1,0:T(8,128)}, bf16[512,1024]{1,0:T(8,128)(2,1)S(1)}, bf16[512,1024]{1,0:T(8,128)(2,1)S(1)}, bf16[512,1024]{1,0:T(8,128)(2,1)S(1)}) custom-call(bf16[512,1024]{1,0:T(8,128)(2,1)} %copy.123.x, bf16[512,1024]{1,0:T(8,128)(2,1)} %copy.124.dy, f32[512,1024]{1,0:T(8,128)} %get-tuple-element.120.spread, ...), custom_call_target="tpu_custom_call" | custom-call | flops 6442450944 | bytes 16777216 | tf_op jit(solution)/shard_map/pallas_call | solution.py:158
  188.2 3.0 add_convert_fusion.2
  191.5 6.9 %shard_map.216 = (bf16[4,3,8,128,128]{4,3,2,1,0:T(8,128)(2,1)}, bf16[4,3,8,128,128]{4,3,2,1,0:T(8,128)(2,1)}) custom-call(bf16[1024,512]{1,0:T(8,128)(2,1)S(1)} %bitcast.198, bf16[1024,512]{1,0:T(8,128)(2,1)S(1)} %get-tuple-element.130.dy_t, bf16[512,1024]{1,0:T(8,128)(2,1)S(1)} %get-tuple-element.108.hg, bf16[512,1024]{1,0:T(8,128)(2,1)} %copy-done.1, ...), custom_call_target="tpu_custom_call" | custom-call | flops 3221225472 | bytes 10485760 | tf_op jit(solution)/shard_map/pallas_call | solution.py:192
  198.4 7.0 %shard_map.217 = (bf16[4,3,8,128,128]{4,3,2,1,0:T(8,128)(2,1)}, bf16[4,3,8,128,128]{4,3,2,1,0:T(8,128)(2,1)}) custom-call(bf16[1024,512]{1,0:T(8,128)(2,1)S(1)} %bitcast.199, bf16[1024,512]{1,0:T(8,128)(2,1)S(1)} %get-tuple-element.130.dy_t, bf16[512,1024]{1,0:T(8,128)(2,1)S(1)} %copy-done.4, bf16[512,1024]{1,0:T(8,128)(2,1)} %copy-done.5, ...), custom_call_target="tpu_custom_call" | custom-call | flops 3221225472 | bytes 10485760 | tf_op jit(solution)/shard_map/pallas_call | solution.py:192
  206.1 13.3 %reduce-scatter.12.cloned.1.call-done = bf16[128,1024]{1,0:T(8,128)(2,1)} async-done(((bf16[512,1024]{1,0:T(8,128)(2,1)}), bf16[128,1024]{1,0:T(8,128)(2,1)}) %reduce-scatter.12.cloned.1.call-update) | async-done | bytes 262160
  222.1 2.5 add_convert_fusion.3
  226.4 1.6 collective-permute-start.18
  229.7 4.1 %add_convert_fusion.1 = bf16[2,3,8,128,128]{4,3,2,1,0:T(8,128)(2,1)} fusion(bf16[4,3,8,128,128]{4,3,2,1,0:T(8,128)(2,1)} %collective-permute-done.31, bf16[4,3,8,128,128]{4,3,2,1,0:T(8,128)(2,1)} %get-tuple-element.111), kind=kLoop, calls=%fused_computation.15 | loop fusion | flops 3145728 | bytes 4718592 | tf_op jit(solution)/shard_map/convert_element_type | solution.py:233
  233.8 1.5 collective-permute-start.32
  235.3 3.3 add_convert_fusion
  238.6 1.5 collective-permute-start.35
  240.0 20.2 %all-gather.8.cloned.1.call-done = bf16[512,1024]{0,1:T(8,128)(2,1)} async-done(((bf16[128,1024]{0,1:T(8,128)(2,1)}), bf16[512,1024]{0,1:T(8,128)(2,1)}) %all-gather.8.cloned.1.call-update) | async-done | bytes 1048592 | tf_op jit(solution)/shard_map/all_gather | solution.py:440
  260.2 1.7 convolution_convert_fusion.4
  262.0 3.1 fusion.17
  268.9 1.4 fusion.16
  272.2 1.9 copy.155
  279.8 1.5 multiply_reduce_fusion
  281.3 1.6 copy.160
  285.6 1.6 collective-permute-start.29
  287.3 5.4 %collective-permute-done.29 = bf16[2,128,384]{2,1,0:T(8,128)(2,1)S(1)} collective-permute-done((bf16[2,128,384]{2,1,0:T(8,128)(2,1)S(1)}, bf16[2,128,384]{2,1,0:T(8,128)(2,1)S(1)}, u32[]{:S(2)}, u32[]{:S(2)}) %collective-permute-start.29) | collective-permute-done | bytes 196640 | tf_op jit(solution)/shard_map/ppermute | solution.py:72
  292.8 1.6 collective-permute-start.26
  294.4 4.8 %collective-permute-done.26 = bf16[2,128,384]{2,1,0:T(8,128)(2,1)S(1)} collective-permute-done((bf16[2,128,384]{2,1,0:T(8,128)(2,1)S(1)}, bf16[2,128,384]{2,1,0:T(8,128)(2,1)S(1)}, u32[]{:S(2)}, u32[]{:S(2)}) %collective-permute-start.26) | collective-permute-done | bytes 196640 | tf_op jit(solution)/shard_map/ppermute | solution.py:72
  299.2 1.6 collective-permute-start.30
  300.9 1.5 collective-permute-start.27
  302.4 2.8 convert_add_fusion.1
  306.1 2.7 convert_add_fusion
  310.8 2.1 collective-permute-start.19
  314.2 9.1 %collective-permute-done.33 = bf16[3,8,128,128]{3,2,1,0:T(8,128)(2,1)S(1)} collective-permute-done((bf16[3,8,128,128]{3,2,1,0:T(8,128)(2,1)S(1)}, bf16[3,8,128,128]{3,2,1,0:T(8,128)(2,1)S(1)}, u32[]{:S(2)}, u32[]{:S(2)}) %collective-permute-start.33) | collective-permute-done | bytes 786464 | tf_op jit(solution)/shard_map/ppermute | solution.py:72
  324.6 1.9 collective-permute-done.36
  328.8 2.4 fusion.35
  332.2 1.8 copy.138.refs_0_
  334.0 2.2 shard_map.215
  336.1 1.5 slice_bitcast_fusion.3
  338.3 3.1 collective-permute-done.21
  341.3 1.5 collective-permute-start.22
  346.1 2.6 collective-permute-done.23
  350.3 2.9 collective-permute-done.24
  (292 shorter events, 62.2 us)
Async XLA Ops:
  7.2 10.4 %copy-start.52 = (bf16[128,128]{1,0:T(8,128)(2,1)S(1)}, bf16[128,128]{1,0:T(8,128)(2,1)}, u32[]{:S(2)}) copy-start(bf16[128,128]{1,0:T(8,128)(2,1)} %param.17) | copy-start | bytes 98308
  7.2 10.4 %copy-start.49 = (bf16[128,256]{1,0:T(8,128)(2,1)S(1)}, bf16[128,256]{1,0:T(8,128)(2,1)}, u32[]{:S(2)}) copy-start(bf16[128,256]{1,0:T(8,128)(2,1)} %param.18) | copy-start | bytes 196612
  7.2 12.0 %copy-start.35 = (bf16[16,128,128]{2,1,0:T(8,128)(2,1)S(1)}, bf16[16,128,128]{2,1,0:T(8,128)(2,1)}, u32[]{:S(2)}) copy-start(bf16[16,128,128]{2,1,0:T(8,128)(2,1)} %param.20) | copy-start | bytes 1572868
  7.2 12.0 %copy-start.36 = (bf16[16,128,128]{2,1,0:T(8,128)(2,1)S(1)}, bf16[16,128,128]{2,1,0:T(8,128)(2,1)}, u32[]{:S(2)}) copy-start(bf16[16,128,128]{2,1,0:T(8,128)(2,1)} %param.21) | copy-start | bytes 1572868
  7.2 41.0 %all-gather.4.cloned.1.call-start = ((), (), s32[]{:S(2)}) async-start(), calls=%async_computation.3 | async-start | bytes 1310720 | tf_op jit(solution)/shard_map/all_gather | solution.py:328
  9.0 10.6 %collective-permute-start.3 = (bf16[128,384]{1,0:T(8,128)(2,1)S(1)}, bf16[128,384]{1,0:T(8,128)(2,1)S(1)}, u32[]{:S(2)}, u32[]{:S(2)}) collective-permute-start(bf16[128,384]{1,0:T(8,128)(2,1)S(1)} %constant_dynamic-update-slice_fusion.2), channel_id=1, source_target_pairs={{0,8},{4,12},{8,0},{12,4},{16,24},{20,28},{24,16},{28,20},{1,9},{5... | collective-permute-start | bytes 294920 | tf_op jit(solution)/shard_map/ppermute | solution.py:72
  17.5 65.5 %reduce-scatter.10.cloned.1.call-start = ((), (), s32[]{:S(2)}) async-start(), calls=%async_computation.6 | async-start | bytes 1310720
  17.6 5.4 %collective-permute-start = (bf16[128,384]{1,0:T(8,128)(2,1)S(1)}, bf16[128,384]{1,0:T(8,128)(2,1)S(1)}, u32[]{:S(2)}, u32[]{:S(2)}) collective-permute-start(bf16[128,384]{1,0:T(8,128)(2,1)S(1)} %constant_dynamic-update-slice_fusion), channel_id=1, source_target_pairs={{0,16},{4,20},{8,24},{12,28},{16,0},{20,4},{24,8},{28,12},{1,17},{... | collective-permute-start | bytes 294920 | tf_op jit(solution)/shard_map/ppermute | solution.py:72
  19.6 6.9 %collective-permute-start.4 = (bf16[2,128,384]{2,1,0:T(8,128)(2,1)S(1)}, bf16[2,128,384]{2,1,0:T(8,128)(2,1)S(1)}, u32[]{:S(2)}, u32[]{:S(2)}) collective-permute-start(bf16[2,128,384]{2,1,0:T(8,128)(2,1)S(1)} %get-tuple-element.161), channel_id=1, source_target_pairs={{0,16},{4,20},{8,24},{12,28},{16,0},{20,4},{24,8},{28,12},{1,17},{... | collective-permute-start | bytes 589832 | tf_op jit(solution)/shard_map/ppermute | solution.py:72
  23.1 5.7 %collective-permute-start.1 = (bf16[2,128,384]{2,1,0:T(8,128)(2,1)S(1)}, bf16[2,128,384]{2,1,0:T(8,128)(2,1)S(1)}, u32[]{:S(2)}, u32[]{:S(2)}) collective-permute-start(bf16[2,128,384]{2,1,0:T(8,128)(2,1)S(1)} %get-tuple-element.163), channel_id=1, source_target_pairs={{0,8},{4,12},{8,0},{12,4},{16,24},{20,28},{24,16},{28,20},{1,9},{5... | collective-permute-start | bytes 589832 | tf_op jit(solution)/shard_map/ppermute | solution.py:72
  26.5 2.7 collective-permute-start.5
  28.9 1.8 collective-permute-start.2
  29.4 20.6 %copy-start.13 = (bf16[4,2,128,384]{3,2,1,0:T(8,128)(2,1)}, bf16[4,2,128,384]{3,2,1,0:T(8,128)(2,1)S(1)}, u32[]{:S(2)}) copy-start(bf16[4,2,128,384]{3,2,1,0:T(8,128)(2,1)S(1)} %pad_maximum_fusion.10) | copy-start | bytes 2359300
  30.8 24.4 %copy-start.16 = (bf16[4,2,128,384]{3,2,1,0:T(8,128)(2,1)}, bf16[4,2,128,384]{3,2,1,0:T(8,128)(2,1)S(1)}, u32[]{:S(2)}) copy-start(bf16[4,2,128,384]{3,2,1,0:T(8,128)(2,1)S(1)} %pad_maximum_fusion.7) | copy-start | bytes 2359300
  57.4 91.3 %all-gather.6.cloned.1.call-start = ((), (), s32[]{:S(2)}) async-start(), calls=%async_computation.4 | async-start | bytes 1310720 | tf_op jit(solution)/shard_map/all_gather | solution.py:381
  57.4 18.3 %collective-permute-start.9 = (bf16[3,8,128,128]{3,2,1,0:T(8,128)(2,1)S(1)}, bf16[3,8,128,128]{3,2,1,0:T(8,128)(2,1)S(1)}, u32[]{:S(2)}, u32[]{:S(2)}) collective-permute-start(bf16[3,8,128,128]{3,2,1,0:T(8,128)(2,1)S(1)} %get-tuple-element.95), channel_id=1, source_target_pairs={{0,8},{4,12},{8,0},{12,4},{16,24},{20,28},{24,16},{28,20},{1,9},{5... | collective-permute-start | bytes 2359304 | tf_op jit(solution)/shard_map/ppermute | solution.py:72
  57.9 20.8 %collective-permute-start.10 = (bf16[3,8,128,128]{3,2,1,0:T(8,128)(2,1)S(1)}, bf16[3,8,128,128]{3,2,1,0:T(8,128)(2,1)S(1)}, u32[]{:S(2)}, u32[]{:S(2)}) collective-permute-start(bf16[3,8,128,128]{3,2,1,0:T(8,128)(2,1)S(1)} %get-tuple-element.96), channel_id=1, source_target_pairs={{0,16},{4,20},{8,24},{12,28},{16,0},{20,4},{24,8},{28,12},{1,17},{... | collective-permute-start | bytes 2359304 | tf_op jit(solution)/shard_map/ppermute | solution.py:72
  77.0 36.0 %collective-permute-start.11 = (bf16[2,3,8,128,128]{4,3,2,1,0:T(8,128)(2,1)}, bf16[2,3,8,128,128]{4,3,2,1,0:T(8,128)(2,1)}, u32[]{:S(2)}, u32[]{:S(2)}) collective-permute-start(bf16[2,3,8,128,128]{4,3,2,1,0:T(8,128)(2,1)} %pad_maximum_fusion.pair), channel_id=1, source_target_pairs={{0,16},{4,20},{8,24},{12,28},{16,0},{20,4},{24,8},{28,12},{1,17},{... | collective-permute-start | bytes 4718600 | tf_op jit(solution)/shard_map/ppermute | solution.py:72
  78.8 37.5 %copy-start.29 = (bf16[128,1024]{1,0:T(8,128)(2,1)S(1)}, bf16[128,1024]{1,0:T(8,128)(2,1)}, u32[]{:S(2)}) copy-start(bf16[128,1024]{1,0:T(8,128)(2,1)} %get-tuple-element.94) | copy-start | bytes 786436
  78.8 50.0 %copy-start.53 = (f32[512,8]{0,1:T(8,128)S(1)}, f32[512,8]{0,1:T(8,128)}, u32[]{:S(2)}) copy-start(f32[512,8]{0,1:T(8,128)} %param.24) | copy-start | bytes 49156
  78.8 50.0 %copy-start.54 = (s32[512,8]{0,1:T(8,128)S(1)}, s32[512,8]{0,1:T(8,128)}, u32[]{:S(2)}) copy-start(s32[512,8]{0,1:T(8,128)} %param.23) | copy-start | bytes 49156
  80.1 35.7 %collective-permute-start.12 = (bf16[2,3,8,128,128]{4,3,2,1,0:T(8,128)(2,1)}, bf16[2,3,8,128,128]{4,3,2,1,0:T(8,128)(2,1)}, u32[]{:S(2)}, u32[]{:S(2)}) collective-permute-start(bf16[2,3,8,128,128]{4,3,2,1,0:T(8,128)(2,1)} %pad_maximum_fusion.1.pair), channel_id=1, source_target_pairs={{0,8},{4,12},{8,0},{12,4},{16,24},{20,28},{24,16},{28,20},{1,9},{5... | collective-permute-start | bytes 4718600 | tf_op jit(solution)/shard_map/ppermute | solution.py:72
  84.1 46.0 %copy-start.9 = (bf16[128,1024]{0,1:T(8,128)(2,1)}, bf16[128,1024]{0,1:T(8,128)(2,1)S(1)}, u32[]{:S(2)}) copy-start(bf16[128,1024]{0,1:T(8,128)(2,1)S(1)} %copy.157) | copy-start | bytes 786436
  84.8 44.0 %copy-start.56 = (f32[128]{0:T(128)}, f32[128]{0:T(128)S(1)}, u32[]{:S(2)}) copy-start(f32[128]{0:T(128)S(1)} %get-tuple-element.169) | copy-start | bytes 1540
  85.7 133.7 %reduce-scatter.12.cloned.1.call-start = ((), (), s32[]{:S(2)}) async-start(), calls=%async_computation.7 | async-start | bytes 1310720
  115.7 35.2 %collective-permute-start.13 = (bf16[2,3,8,128,128]{4,3,2,1,0:T(8,128)(2,1)}, bf16[2,3,8,128,128]{4,3,2,1,0:T(8,128)(2,1)}, u32[]{:S(2)}, u32[]{:S(2)}) collective-permute-start(bf16[2,3,8,128,128]{4,3,2,1,0:T(8,128)(2,1)} %pad_maximum_fusion.pair), channel_id=1, source_target_pairs={{0,4},{4,0},{8,12},{12,8},{16,20},{20,16},{24,28},{28,24},{1,5},{5... | collective-permute-start | bytes 4718600 | tf_op jit(solution)/shard_map/ppermute | solution.py:72
  115.7 35.2 %collective-permute-start.14 = (bf16[2,3,8,128,128]{4,3,2,1,0:T(8,128)(2,1)}, bf16[2,3,8,128,128]{4,3,2,1,0:T(8,128)(2,1)}, u32[]{:S(2)}, u32[]{:S(2)}) collective-permute-start(bf16[2,3,8,128,128]{4,3,2,1,0:T(8,128)(2,1)} %collective-permute-done.11.second), channel_id=1, source_target_pairs={{0,4},{4,0},{8,12},{12,8},{16,20},{20,16},{24,28},{28,24},{1,5},{5... | collective-permute-start | bytes 4718600 | tf_op jit(solution)/shard_map/ppermute | solution.py:72
  116.3 12.5 %collective-permute-start.6 = (bf16[128,1024]{1,0:T(8,128)(2,1)S(1)}, bf16[128,1024]{1,0:T(8,128)(2,1)S(1)}, u32[]{:S(2)}, u32[]{:S(2)}) collective-permute-start(bf16[128,1024]{1,0:T(8,128)(2,1)S(1)} %copy-done.29), channel_id=1, source_target_pairs={{0,1},{1,0},{2,3},{3,2},{4,5},{5,4},{6,7},{7,6},{8,9},{9,8},{10,11... | collective-permute-start | bytes 786440 | tf_op jit(solution)/shard_map/ppermute | solution.py:72
  116.3 17.8 %collective-permute-start.7 = (bf16[128,1024]{1,0:T(8,128)(2,1)S(1)}, bf16[128,1024]{1,0:T(8,128)(2,1)S(1)}, u32[]{:S(2)}, u32[]{:S(2)}) collective-permute-start(bf16[128,1024]{1,0:T(8,128)(2,1)S(1)} %copy-done.29), channel_id=1, source_target_pairs={{0,2},{1,3},{2,0},{3,1},{4,6},{5,7},{6,4},{7,5},{8,10},{9,11},{10,... | collective-permute-start | bytes 786440 | tf_op jit(solution)/shard_map/ppermute | solution.py:72
  118.1 50.3 %collective-permute-start.15 = (bf16[2,3,8,128,128]{4,3,2,1,0:T(8,128)(2,1)}, bf16[2,3,8,128,128]{4,3,2,1,0:T(8,128)(2,1)}, u32[]{:S(2)}, u32[]{:S(2)}) collective-permute-start(bf16[2,3,8,128,128]{4,3,2,1,0:T(8,128)(2,1)} %pad_maximum_fusion.1.pair), channel_id=1, source_target_pairs={{0,4},{4,0},{8,12},{12,8},{16,20},{20,16},{24,28},{28,24},{1,5},{5... | collective-permute-start | bytes 4718600 | tf_op jit(solution)/shard_map/ppermute | solution.py:72
  128.7 39.7 %collective-permute-start.16 = (bf16[2,3,8,128,128]{4,3,2,1,0:T(8,128)(2,1)}, bf16[2,3,8,128,128]{4,3,2,1,0:T(8,128)(2,1)}, u32[]{:S(2)}, u32[]{:S(2)}) collective-permute-start(bf16[2,3,8,128,128]{4,3,2,1,0:T(8,128)(2,1)} %collective-permute-done.12.second), channel_id=1, source_target_pairs={{0,4},{4,0},{8,12},{12,8},{16,20},{20,16},{24,28},{28,24},{1,5},{5... | collective-permute-start | bytes 4718600 | tf_op jit(solution)/shard_map/ppermute | solution.py:72
  134.1 10.6 %collective-permute-start.8 = (bf16[128,1024]{1,0:T(8,128)(2,1)S(1)}, bf16[128,1024]{1,0:T(8,128)(2,1)S(1)}, u32[]{:S(2)}, u32[]{:S(2)}) collective-permute-start(bf16[128,1024]{1,0:T(8,128)(2,1)S(1)} %copy-done.29), channel_id=1, source_target_pairs={{0,3},{1,2},{2,1},{3,0},{4,7},{5,6},{6,5},{7,4},{8,11},{9,10},{10,... | collective-permute-start | bytes 786440 | tf_op jit(solution)/shard_map/ppermute | solution.py:72
  168.4 16.8 %copy-start.1 = (bf16[512,1024]{1,0:T(8,128)(2,1)}, bf16[512,1024]{1,0:T(8,128)(2,1)S(1)}, u32[]{:S(2)}) copy-start(bf16[512,1024]{1,0:T(8,128)(2,1)S(1)} %get-tuple-element.109.gg) | copy-start | bytes 3145732
  168.4 19.8 %copy-start.23 = (f32[512,1024]{1,0:T(8,128)S(1)}, f32[512,1024]{1,0:T(8,128)}, u32[]{:S(2)}) copy-start(f32[512,1024]{1,0:T(8,128)} %get-tuple-element.103) | copy-start | bytes 6291460
  191.2 69.0 %all-gather.8.cloned.1.call-start = ((), (), s32[]{:S(2)}) async-start(), calls=%async_computation.5 | async-start | bytes 1310720 | tf_op jit(solution)/shard_map/all_gather | solution.py:440
  198.4 31.3 %collective-permute-start.31 = (bf16[4,3,8,128,128]{4,3,2,1,0:T(8,128)(2,1)}, bf16[4,3,8,128,128]{4,3,2,1,0:T(8,128)(2,1)}, u32[]{:S(2)}, u32[]{:S(2)}) collective-permute-start(bf16[4,3,8,128,128]{4,3,2,1,0:T(8,128)(2,1)} %get-tuple-element.112), channel_id=1, source_target_pairs={{0,4},{4,0},{8,12},{12,8},{16,20},{20,16},{24,28},{28,24},{1,5},{5... | collective-permute-start | bytes 9437192 | tf_op jit(solution)/shard_map/ppermute | solution.py:72
  198.4 7.5 %copy-start.30 = (bf16[128,1024]{1,0:T(8,128)(2,1)S(1)}, bf16[128,1024]{1,0:T(8,128)(2,1)}, u32[]{:S(2)}) copy-start(bf16[128,1024]{1,0:T(8,128)(2,1)} %get-tuple-element.94) | copy-start | bytes 786436
  198.4 22.1 %copy-start.10 = (bf16[128,1024]{0,1:T(8,128)(2,1)S(1)}, bf16[128,1024]{0,1:T(8,128)(2,1)}, u32[]{:S(2)}) copy-start(bf16[128,1024]{0,1:T(8,128)(2,1)} %copy-done.9) | copy-start | bytes 786436
  198.4 22.1 %copy-start.57 = (f32[128]{0:T(128)S(1)}, f32[128]{0:T(128)}, u32[]{:S(2)}) copy-start(f32[128]{0:T(128)} %copy-done.56) | copy-start | bytes 1540
  198.4 22.6 %copy-start.61 = (f32[128]{0:T(128)S(1)}, f32[128]{0:T(128)}, u32[]{:S(2)}) copy-start(f32[128]{0:T(128)} %get-tuple-element.168) | copy-start | bytes 1540
  205.4 16.6 %copy-start.51 = (f32[2,2,512]{2,1,0:T(2,128)S(1)}, f32[2,2,512]{2,1,0:T(2,128)}, u32[]{:S(2)}) copy-start(f32[2,2,512]{2,1,0:T(2,128)} %copy-done.50) | copy-start | bytes 24580
  205.4 29.8 %collective-permute-start.34 = (bf16[4,3,8,128,128]{4,3,2,1,0:T(8,128)(2,1)}, bf16[4,3,8,128,128]{4,3,2,1,0:T(8,128)(2,1)}, u32[]{:S(2)}, u32[]{:S(2)}) collective-permute-start(bf16[4,3,8,128,128]{4,3,2,1,0:T(8,128)(2,1)} %get-tuple-element.117), channel_id=1, source_target_pairs={{0,4},{4,0},{8,12},{12,8},{16,20},{20,16},{24,28},{28,24},{1,5},{5... | collective-permute-start | bytes 9437192 | tf_op jit(solution)/shard_map/ppermute | solution.py:72
  206.1 18.5 %copy-start.21 = (bf16[128,1024]{0,1:T(8,128)(2,1)}, bf16[128,1024]{0,1:T(8,128)(2,1)S(1)}, u32[]{:S(2)}) copy-start(bf16[128,1024]{0,1:T(8,128)(2,1)S(1)} %copy.131) | copy-start | bytes 786436
  222.0 104.7 %reduce-scatter.14.cloned.1.call-start = ((), (), s32[]{:S(2)}) async-start(), calls=%async_computation.8 | async-start | bytes 1310720
  225.6 102.4 %collective-permute-start.17 = (bf16[128,1024]{0,1:T(8,128)(2,1)}, bf16[128,1024]{0,1:T(8,128)(2,1)}, u32[]{:S(2)}, u32[]{:S(2)}) collective-permute-start(bf16[128,1024]{0,1:T(8,128)(2,1)} %bitcast.49), channel_id=1, source_target_pairs={{0,1},{1,0},{2,3},{3,2},{4,5},{5,4},{6,7},{7,6},{8,9},{9,8},{10,11... | collective-permute-start | bytes 786440 | tf_op jit(solution)/shard_map/ppermute | solution.py:72
  226.4 101.6 %collective-permute-start.18 = (bf16[128,1024]{0,1:T(8,128)(2,1)}, bf16[128,1024]{0,1:T(8,128)(2,1)}, u32[]{:S(2)}, u32[]{:S(2)}) collective-permute-start(bf16[128,1024]{0,1:T(8,128)(2,1)} %bitcast.50), channel_id=1, source_target_pairs={{0,2},{1,3},{2,0},{3,1},{4,6},{5,7},{6,4},{7,5},{8,10},{9,11},{10,... | collective-permute-start | bytes 786440 | tf_op jit(solution)/shard_map/ppermute | solution.py:72
  233.8 67.1 %collective-permute-start.32 = (bf16[2,3,8,128,128]{4,3,2,1,0:T(8,128)(2,1)}, bf16[2,3,8,128,128]{4,3,2,1,0:T(8,128)(2,1)}, u32[]{:S(2)}, u32[]{:S(2)}) collective-permute-start(bf16[2,3,8,128,128]{4,3,2,1,0:T(8,128)(2,1)} %add_convert_fusion.1), channel_id=1, source_target_pairs={{0,8},{4,12},{8,0},{12,4},{16,24},{20,28},{24,16},{28,20},{1,9},{5... | collective-permute-start | bytes 4718600 | tf_op jit(solution)/shard_map/ppermute | solution.py:72
  235.3 25.0 %copy-start.17 = (bf16[4,2,128,384]{3,2,1,0:T(8,128)(2,1)S(1)}, bf16[4,2,128,384]{3,2,1,0:T(8,128)(2,1)}, u32[]{:S(2)}) copy-start(bf16[4,2,128,384]{3,2,1,0:T(8,128)(2,1)} %copy-done.16) | copy-start | bytes 2359300
  238.6 66.9 %collective-permute-start.35 = (bf16[2,3,8,128,128]{4,3,2,1,0:T(8,128)(2,1)}, bf16[2,3,8,128,128]{4,3,2,1,0:T(8,128)(2,1)}, u32[]{:S(2)}, u32[]{:S(2)}) collective-permute-start(bf16[2,3,8,128,128]{4,3,2,1,0:T(8,128)(2,1)} %add_convert_fusion), channel_id=1, source_target_pairs={{0,16},{4,20},{8,24},{12,28},{16,0},{20,4},{24,8},{28,12},{1,17},{... | collective-permute-start | bytes 4718600 | tf_op jit(solution)/shard_map/ppermute | solution.py:72
  274.1 9.4 %collective-permute-start.28 = (bf16[2,2,128,384]{3,2,1,0:T(8,128)(2,1)}, bf16[2,2,128,384]{3,2,1,0:T(8,128)(2,1)}, u32[]{:S(2)}, u32[]{:S(2)}) collective-permute-start(bf16[2,2,128,384]{3,2,1,0:T(8,128)(2,1)} %bitcast.242), channel_id=1, source_target_pairs={{0,4},{4,0},{8,12},{12,8},{16,20},{20,16},{24,28},{28,24},{1,5},{5... | collective-permute-start | bytes 1179656 | tf_op jit(solution)/shard_map/ppermute | solution.py:72
  283.5 2.1 collective-permute-start.25
  285.1 17.4 %copy-start.20 = (bf16[4,3,8,128,128]{4,3,2,1,0:T(8,128)(2,1)S(1)}, bf16[4,3,8,128,128]{4,3,2,1,0:T(8,128)(2,1)}, u32[]{:S(2)}) copy-start(bf16[4,3,8,128,128]{4,3,2,1,0:T(8,128)(2,1)} %get-tuple-element.111) | copy-start | bytes 9437188
  285.6 7.2 %collective-permute-start.29 = (bf16[2,128,384]{2,1,0:T(8,128)(2,1)S(1)}, bf16[2,128,384]{2,1,0:T(8,128)(2,1)S(1)}, u32[]{:S(2)}, u32[]{:S(2)}) collective-permute-start(bf16[2,128,384]{2,1,0:T(8,128)(2,1)S(1)} %slice_bitcast_fusion.14), channel_id=1, source_target_pairs={{0,16},{4,20},{8,24},{12,28},{16,0},{20,4},{24,8},{28,12},{1,17},{... | collective-permute-start | bytes 589832 | tf_op jit(solution)/shard_map/ppermute | solution.py:72
  292.8 6.5 %collective-permute-start.26 = (bf16[2,128,384]{2,1,0:T(8,128)(2,1)S(1)}, bf16[2,128,384]{2,1,0:T(8,128)(2,1)S(1)}, u32[]{:S(2)}, u32[]{:S(2)}) collective-permute-start(bf16[2,128,384]{2,1,0:T(8,128)(2,1)S(1)} %slice_bitcast_fusion.16), channel_id=1, source_target_pairs={{0,8},{4,12},{8,0},{12,4},{16,24},{20,28},{24,16},{28,20},{1,9},{5... | collective-permute-start | bytes 589832 | tf_op jit(solution)/shard_map/ppermute | solution.py:72
  299.2 9.7 %collective-permute-start.30 = (bf16[128,384]{1,0:T(8,128)(2,1)S(1)}, bf16[128,384]{1,0:T(8,128)(2,1)S(1)}, u32[]{:S(2)}, u32[]{:S(2)}) collective-permute-start(bf16[128,384]{1,0:T(8,128)(2,1)S(1)} %slice_bitcast_fusion.18), channel_id=1, source_target_pairs={{0,8},{4,12},{8,0},{12,4},{16,24},{20,28},{24,16},{28,20},{1,9},{5... | collective-permute-start | bytes 294920 | tf_op jit(solution)/shard_map/ppermute | solution.py:72
  300.9 9.9 %collective-permute-start.27 = (bf16[128,384]{1,0:T(8,128)(2,1)S(1)}, bf16[128,384]{1,0:T(8,128)(2,1)S(1)}, u32[]{:S(2)}, u32[]{:S(2)}) collective-permute-start(bf16[128,384]{1,0:T(8,128)(2,1)S(1)} %slice_bitcast_fusion.20), channel_id=1, source_target_pairs={{0,16},{4,20},{8,24},{12,28},{16,0},{20,4},{24,8},{28,12},{1,17},{... | collective-permute-start | bytes 294920 | tf_op jit(solution)/shard_map/ppermute | solution.py:72
  305.4 17.8 %collective-permute-start.33 = (bf16[3,8,128,128]{3,2,1,0:T(8,128)(2,1)S(1)}, bf16[3,8,128,128]{3,2,1,0:T(8,128)(2,1)S(1)}, u32[]{:S(2)}, u32[]{:S(2)}) collective-permute-start(bf16[3,8,128,128]{3,2,1,0:T(8,128)(2,1)S(1)} %fusion.20), channel_id=1, source_target_pairs={{0,16},{4,20},{8,24},{12,28},{16,0},{20,4},{24,8},{28,12},{1,17},{... | collective-permute-start | bytes 2359304 | tf_op jit(solution)/shard_map/ppermute | solution.py:72
  308.9 17.5 %collective-permute-start.36 = (bf16[3,8,128,128]{3,2,1,0:T(8,128)(2,1)S(1)}, bf16[3,8,128,128]{3,2,1,0:T(8,128)(2,1)S(1)}, u32[]{:S(2)}, u32[]{:S(2)}) collective-permute-start(bf16[3,8,128,128]{3,2,1,0:T(8,128)(2,1)S(1)} %fusion.21), channel_id=1, source_target_pairs={{0,8},{4,12},{8,0},{12,4},{16,24},{20,28},{24,16},{28,20},{1,9},{5... | collective-permute-start | bytes 2359304 | tf_op jit(solution)/shard_map/ppermute | solution.py:72
  310.8 17.3 %collective-permute-start.19 = (bf16[128,1024]{0,1:T(8,128)(2,1)S(1)}, bf16[128,1024]{0,1:T(8,128)(2,1)S(1)}, u32[]{:S(2)}, u32[]{:S(2)}) collective-permute-start(bf16[128,1024]{0,1:T(8,128)(2,1)S(1)} %bitcast.244), channel_id=1, source_target_pairs={{0,3},{1,2},{2,1},{3,0},{4,7},{5,6},{6,5},{7,4},{8,11},{9,10},{10,... | collective-permute-start | bytes 786440 | tf_op jit(solution)/shard_map/ppermute | solution.py:72
  336.1 1.5 collective-permute-start.20
  337.6 3.7 %collective-permute-start.21 = (f32[2,1024]{1,0:T(2,128)S(1)}, f32[2,1024]{1,0:T(2,128)S(1)}, u32[]{:S(2)}, u32[]{:S(2)}) collective-permute-start(f32[2,1024]{1,0:T(2,128)S(1)} %add.179), channel_id=1, source_target_pairs={{0,8},{4,12},{8,0},{12,4},{16,24},{20,28},{24,16},{28,20},{1,9},{5... | collective-permute-start | bytes 24584 | tf_op jit(solution)/shard_map/ppermute | solution.py:72
  341.3 3.7 %collective-permute-start.22 = (f32[2,1024]{1,0:T(2,128)S(1)}, f32[2,1024]{1,0:T(2,128)S(1)}, u32[]{:S(2)}, u32[]{:S(2)}) collective-permute-start(f32[2,1024]{1,0:T(2,128)S(1)} %add.180), channel_id=1, source_target_pairs={{0,16},{4,20},{8,24},{12,28},{16,0},{20,4},{24,8},{28,12},{1,17},{... | collective-permute-start | bytes 24584 | tf_op jit(solution)/shard_map/ppermute | solution.py:72
  345.0 3.7 %collective-permute-start.23 = (f32[2,1024]{1,0:T(2,128)S(1)}, f32[2,1024]{1,0:T(2,128)S(1)}, u32[]{:S(2)}, u32[]{:S(2)}) collective-permute-start(f32[2,1024]{1,0:T(2,128)S(1)} %add.181), channel_id=1, source_target_pairs={{0,1},{1,0},{2,3},{3,2},{4,5},{5,4},{6,7},{7,6},{8,9},{9,8},{10,11... | collective-permute-start | bytes 24584 | tf_op jit(solution)/shard_map/ppermute | solution.py:72
  348.7 4.5 %collective-permute-start.24 = (f32[2,1024]{1,0:T(2,128)S(1)}, f32[2,1024]{1,0:T(2,128)S(1)}, u32[]{:S(2)}, u32[]{:S(2)}) collective-permute-start(f32[2,1024]{1,0:T(2,128)S(1)} %add.182), channel_id=1, source_target_pairs={{0,2},{1,3},{2,0},{3,1},{4,6},{5,7},{6,4},{7,5},{8,10},{9,11},{10,... | collective-permute-start | bytes 24584 | tf_op jit(solution)/shard_map/ppermute | solution.py:72
  (45 other events, 123.4 us)
Sparse Core Ops, SparseCore 0:
  17.6 30.5 all-gather.3
  57.5 25.4 reduce-scatter.9
  85.8 28.8 all-gather.5
  191.3 28.0 reduce-scatter.11
  222.1 38.0 all-gather.7
  283.0 26.9 reduce-scatter.13
where the time goes:
time: 367 us; the launch traced here: 361 us
  waiting for transfers between devices  153 us (42%)
  Pallas kernels  51.3 us (14%)
  local copies, waits for them, and re-layouts  46.6 us (13%)
  other arithmetic  43.2 us (12%)
  starting transfers between devices  33.7 us (9%)
  matrix products  17.7 us (5%)
  between operations  15.8 us (4%)
    ppermute x37, waiting for transfers between devices, swap(): return lax.ppermute(value, axis, [(i, i ^ bit) for i in range(size)])  100 us
    pallas_call x2, Pallas kernels, experts_part(): pl.pallas_call(functools.partial(experts_kernel, way), grid=(half // 2,),...  33.2 us
    ppermute x37, starting transfers between devices, swap(): return lax.ppermute(value, axis, [(i, i ^ bit) for i in range(size)])  33.1 us
    all_gather x1, waiting for transfers between devices, local(): lax.all_gather(middle_grad.astype(bf_type), 'tensor', axis=0, tiled=True)  20.2 us
    unnamed x140, local copies, waits for them, and re-layouts  18.7 us
    all_gather x1, waiting for transfers between devices, local(): lax.all_gather((residual * factor_one * gain_one).astype(bf_type), 'tenso...  17.4 us
    unnamed x9, waiting for transfers between devices  14.9 us
    pallas_call x2, Pallas kernels, weight_grads(): pl.pallas_call(functools.partial(weight_grads_kernel, way), grid=(half //...  13.9 us
  transfers between devices with their start and end apart: 43, of which 22 were waited for; matrix products, arithmetic and copies ran while one was open for 23% of the time, Pallas kernels for 9%

commit v1 on v0

--- a/solution.py
+++ b/solution.py
@@ -110,7 +110,7 @@
 
 
 def experts_kernel(
-    way, x, dy, spread, pair, second, pair_o, second_o, n2, mixed, hg, gg, ug, wg, wu, wd
+    way, x, dy, mixing, pair, second, pair_o, second_o, n2, mixed, hg, gg, ug, wg, wu, wd
 ):
     pieces = (pair, second, pair_o, second_o)
     for core in range(2):
@@ -121,12 +121,20 @@
                 for k, weight in enumerate((wg, wu, wd)):
                     for e in range(2):
                         weight[rows, e * 128 : (e + 1) * 128] = pieces[core * 2 + late][j, k, e]
+    step = pl.program_id(0)
+    lanes = lax.broadcasted_iota(jnp.int32, mixing.shape, 1)
+    taken = []
+    for e in range(2):
+        expert = way * 2 * pl.num_programs(0) + 2 * step + e
+        column = jnp.sum(jnp.where(lanes == expert, mixing[...], 0.0), axis=1, keepdims=True)
+        taken.append(jnp.broadcast_to(column, (column.shape[0], 128)))
+    spread = jnp.concatenate(taken, axis=1)
     gate_proj = mm(x[...], wg[...])
     up_proj = mm(x[...], wu[...])
-    hidden_grad = mm(dy[...], wd[...]) * spread[...]
+    hidden_grad = mm(dy[...], wd[...]) * spread
     sigmoid_g = 1.0 / (1.0 + jnp.exp(-gate_proj))
     activated = gate_proj * sigmoid_g
-    hidden = (activated * up_proj * spread[...]).astype(BF)
+    hidden = (activated * up_proj * spread).astype(BF)
     gate_grad = (
         hidden_grad * up_proj * sigmoid_g * (1.0 + gate_proj * (1.0 - sigmoid_g))
     ).astype(BF)
@@ -148,17 +156,18 @@
         mixed[...] += mixed_step
 
 
-def experts_part(way, x, dy, spread, pieces):
+def experts_part(way, x, dy, mixing, pieces):
     rows, width = x.shape
     half = pieces[0].shape[2]
     whole = pl.BlockSpec((rows, width), lambda i: (0, 0))
     tile = pl.BlockSpec((rows, 256), lambda i: (0, i))
+    gates = pl.BlockSpec(mixing.shape, lambda i: (0, 0))
     piece = pl.BlockSpec((2, 3, 2, 128, 128), lambda i: (0, 0, i, 0, 0))
     hidden_shape = jax.ShapeDtypeStruct((rows, half * 128), BF)
     return pl.pallas_call(
         functools.partial(experts_kernel, way),
         grid=(half // 2,),
-        in_specs=[whole, whole, tile, piece, piece, piece, piece],
+        in_specs=[whole, whole, gates, piece, piece, piece, piece],
         out_specs=[whole, whole, tile, tile, tile],
         out_shape=[jax.ShapeDtypeStruct((rows, width), F32)] * 2 + [hidden_shape] * 3,
         scratch_shapes=[pltpu.VMEM((width, 256), BF)] * 3,
@@ -166,27 +175,27 @@
         cost_estimate=pl.CostEstimate(
             flops=12 * rows * width * half * 128, bytes_accessed=16 * 2**20, transcendentals=0
         ),
-    )(x, dy, spread, *pieces)
-
-
-def weight_grads_kernel(way, x_t, dy_t, hg, gg, ug, sent, kept):
-    for k, (left, right) in enumerate(((x_t, gg), (x_t, ug), (dy_t, hg))):
-        grad = mm(left[...], right[...]).astype(BF)
+    )(x, dy, mixing, *pieces)
+
+
+def weight_grads_kernel(way, x, dy, hg, gg, ug, sent, kept):
+    for k, (left, right) in enumerate(((x, gg), (x, ug), (dy, hg))):
+        grad = t_mm(left[...], right[...]).astype(BF)
         for core in range(2):
-            for y in range(2):
-                for x in range(2):
-                    place = core * 4 + y * 2 + x
-                    slot = (1 - x) * 2 + 1 - y if way == 0 else (1 - y) * 2 + 1 - x
+            for i in range(2):
+                for j in range(2):
+                    place = core * 4 + i * 2 + j
+                    slot = (1 - j) * 2 + 1 - i if way == 0 else (1 - i) * 2 + 1 - j
                     for e in range(2):
                         (sent if core else kept)[slot, k, e] = grad[
                             place * 128 : (place + 1) * 128, e * 128 : (e + 1) * 128
                         ]
 
 
-def weight_grads(way, x_t, dy_t, hg, gg, ug):
-    width, rows = x_t.shape
+def weight_grads(way, x, dy, hg, gg, ug):
+    rows, width = x.shape
     half = hg.shape[1] // 128
-    whole = pl.BlockSpec((width, rows), lambda i: (0, 0))
+    whole = pl.BlockSpec((rows, width), lambda i: (0, 0))
     tile = pl.BlockSpec((rows, 256), lambda i: (0, i))
     quad = pl.BlockSpec((4, 3, 2, 128, 128), lambda i: (0, 0, i, 0, 0))
     return pl.pallas_call(
@@ -199,18 +208,22 @@
         cost_estimate=pl.CostEstimate(
             flops=6 * rows * width * half * 128, bytes_accessed=10 * 2**20, transcendentals=0
         ),
-    )(x_t, dy_t, hg, gg, ug)
+    )(x, dy, hg, gg, ug)
 
 
 WAYS = ((2, 4), (4, 2))
 
 
-def sum_pieces(way, sent, kept):
-    near, far = WAYS[way]
+def sum_near(way, sent, kept):
     core = swap(sent, "dp", 1)
-    first = swap(add_low(kept[:2], core[:2]), "dp", near)
-    held = kept[2:].astype(F32) + core[2:].astype(F32) + first.astype(F32)
-    return held[1] + swap(held[0].astype(BF), "dp", far).astype(F32)
+    first = swap(add_low(kept[:2], core[:2]), "dp", WAYS[way][0])
+    return kept[2:], core[2:], first
+
+
+def sum_far(way, terms):
+    kept, core, first = (t.astype(F32) for t in terms)
+    held = kept + core + first
+    return held[1] + swap(held[0].astype(BF), "dp", WAYS[way][1]).astype(F32)
 
 
 def gather_rows(shards):
@@ -332,7 +345,6 @@
     parts = (slice(0, half), slice(half, None))
     if relative:
         shards = [jnp.stack([w_gate[p], w_up[p], w_down[p]]) for p in parts]
-        shards, full_qk = lax.optimization_barrier((shards, full_qk))
         firsts = [swap(w, "dp", way[0]) for w, way in zip(shards, WAYS)]
         pairs = [jnp.stack([w, f]) for w, f in zip(shards, firsts)]
         seconds = [swap(p, "dp", way[1]) for p, way in zip(pairs, WAYS)]
@@ -342,7 +354,8 @@
         ] + [rows_first(w_down[p]) for p in parts]
         shards, full_qk = lax.optimization_barrier((shards, full_qk))
         gu_a, gu_b, d_a, d_b = gather_rows(shards)
-    grad_rows = gather_tokens(cotangent)
+    later, normed = lax.optimization_barrier((cotangent, normed))
+    grad_rows = gather_tokens(later)
     cosine_table, sine_table = rope_tables(LEN, HEAD_SIZE)
     cosine_table = cosine_table[:, None, :]
     sine_table = sine_table[:, None, :]
@@ -383,15 +396,11 @@
     mixing = jnp.sum(jnp.where(chosen, gate_weights[:, :, None], 0.0), axis=1)
     if relative:
         pairs, seconds, _ = lax.optimization_barrier((pairs, seconds, normed_two_rows))
-        spread = jnp.broadcast_to(
-            mixing[:, :, None], (group_rows, experts, 128)
-        ).reshape(group_rows, experts * 128)
         results = []
         for way in range(2):
             pieces = (pairs[way], seconds[way], swap(pairs[way], "dp", 1))
             pieces = pieces + (swap(seconds[way], "dp", 1),)
-            columns = spread[:, way * half * 128 : (way + 1) * half * 128]
-            results.append(experts_part(way, normed_two, grad_rows, columns, pieces))
+            results.append(experts_part(way, normed_two, grad_rows, mixing, pieces))
         normed_two_part = results[0][0] + results[1][0]
         mixed_part = results[0][1] + results[1][1]
     else:
@@ -416,16 +425,11 @@
     normed_two_grad = lax.psum_scatter(
         normed_two_part.astype(bf_type), "tensor", scatter_dimension=0, tiled=True
     ).astype(f_type)
-    residual_out = (middle + scatter_tokens(mixed_part.astype(bf_type))).astype(bf_type)
     if relative:
-        x_t, dy_t = normed_two.T, grad_rows.T
         sums = []
         for way in range(2):
-            sent, kept = weight_grads(way, x_t, dy_t, *results[way][2:])
-            sums.append(sum_pieces(way, sent, kept))
-        w_gate_grad, w_up_grad, w_down_grad = (
-            jnp.concatenate([sums[0][k], sums[1][k]]) for k in range(3)
-        )
+            sent, kept = weight_grads(way, normed_two, grad_rows, *results[way][2:])
+            sums.append(sum_near(way, sent, kept))
     else:
         gu_grads, down_grads = [], []
         for way, (both_grad, hidden) in enumerate(low_grads):
@@ -438,6 +442,8 @@
     back_two, gain_two_part = norm_back(middle, factor_two, gain_two, normed_two_grad)
     middle_grad = cotangent.astype(f_type) + back_two
     middle_rows = lax.all_gather(middle_grad.astype(bf_type), "tensor", axis=0, tiled=True)
+    mixed_low, middle_rows = lax.optimization_barrier((mixed_part.astype(bf_type), middle_rows))
+    residual_out = (middle + scatter_tokens(mixed_low)).astype(bf_type)
     grad_out_w = t_mm(middle_rows, heads_out)
     heads_grad = jnp.dot(middle_rows, full_o, preferred_element_type=f_type).astype(bf_type)
     heads_grad = heads_grad.reshape(sequences, LEN, heads_q * HEAD_SIZE)
@@ -470,6 +476,14 @@
     query_rgrad, keys_rgrad, values_rgrad = lax.map(
         backward_one, (query, key_rows, value_rows, log_sums, heads_grad)
     )
+    if relative:
+        sums, query_rgrad, keys_rgrad, values_rgrad = lax.optimization_barrier(
+            (sums, query_rgrad, keys_rgrad, values_rgrad)
+        )
+        sums = [sum_far(way, sums[way]) for way in range(2)]
+        w_gate_grad, w_up_grad, w_down_grad = (
+            jnp.concatenate([sums[0][k], sums[1][k]]) for k in range(3)
+        )
     query_grad = (
         rotate_back(query_rgrad, cosine_table, sine_table)
         .astype(bf_type)
@@ -490,15 +504,13 @@
     w_value_grad, w_out_grad = grad_vo_w[:, :k_width], grad_vo_w[:, k_width:]
     normed_part = mm_t(qk_grad, full_qk) + mm_t(values_grad, full_v)
     gain_one_part = jnp.sum(normed_part * normed.astype(f_type), axis=0) / gain_one
+    (gains,) = reorder((jnp.stack([gain_one_part, gain_two_part]),), True)
+    gains = total(gains)
     normed_grad = lax.psum_scatter(
         normed_part.astype(bf_type), "tensor", scatter_dimension=0, tiled=True
     ).astype(f_type)
     back_one, _ = norm_back(residual, factor_one, gain_one, normed_grad)
-    gains = jnp.stack([gain_one_part, gain_two_part])
-    residual_out, input_grad, gains = reorder(
-        (residual_out, middle_grad + back_one, gains), True
-    )
-    gains = total(gains)
+    residual_out, input_grad = reorder((residual_out, middle_grad + back_one), True)
     norm1_gain_grad, norm2_gain_grad = gains[0], gains[1]
     return (
         residual_out,

time: 367 us -> 383 us (1.044); the launches traced: 361 us -> 382 us
  waiting for transfers between devices: 153 us -> 177 us
  local copies, waits for them, and re-layouts: 46.6 us -> 34.7 us
  other arithmetic: 43.2 us -> 47.7 us
    ppermute x37, waiting for transfers between devices: 100 us -> 143 us  [swap(): return lax.ppermute(value, axis, [(i, i ^ bit) for i in range(size)])]
    all_gather x1, waiting for transfers between devices: 20.2 us -> 2.59 us  [local(): lax.all_gather(middle_grad.astype(bf_type), 'tensor', axis=0, tiled=True)]
    unnamed x9 -> x6, waiting for transfers between devices: 14.9 us -> 0.1 us
    reduce_scatter x0 -> x3, waiting for transfers between devices: none -> 13.1 us  [the longest x1 10.2 us: local(): lax.psum_scatter(normed_two_part.astype(bf_type), 'tensor', scatter_dimen...]
    unnamed x140 -> x146, local copies, waits for them, and re-layouts: 18.7 us -> 10 us
    slice x1 -> x4, local copies, waits for them, and re-layouts: 4.89 us -> 9.59 us  [sum_near(): return (kept[2:], core[2:], first)]
    dynamic_slice x9 -> x0, local copies, waits for them, and re-layouts: 4.05 us -> none  [the longest x3 2.52 us: scatter_tokens(): piece = lax.dynamic_index_in_dim(blocks, me ^ r, 0, keepdims=False)]
  transfers between devices with their start and end apart: 43 -> 43, of which waited for: 22 -> 23; matrix products, arithmetic and copies ran while one was open for 23% -> 21% of each run, Pallas kernels for 9% -> 9%
where the time goes in v1:
time: 383 us; the launch traced here: 382 us
  waiting for transfers between devices  177 us (46%)
  Pallas kernels  52.6 us (14%)
  other arithmetic  47.7 us (12%)
  starting transfers between devices  36.5 us (10%)
  local copies, waits for them, and re-layouts  34.7 us (9%)
  matrix products  18.5 us (5%)
  between operations  15.3 us (4%)
    ppermute x37, waiting for transfers between devices, swap(): return lax.ppermute(value, axis, [(i, i ^ bit) for i in range(size)])  143 us
    ppermute x37, starting transfers between devices, swap(): return lax.ppermute(value, axis, [(i, i ^ bit) for i in range(size)])  35.9 us
    pallas_call x2, Pallas kernels, experts_part(): pl.pallas_call(functools.partial(experts_kernel, way), grid=(half // 2,),...  32.9 us
    all_gather x1, waiting for transfers between devices, local(): lax.all_gather((residual * factor_one * gain_one).astype(bf_type), 'tenso...  18.1 us
    pallas_call x2, Pallas kernels, weight_grads(): pl.pallas_call(functools.partial(weight_grads_kernel, way), grid=(half //...  14.3 us
    reduce_scatter x1, waiting for transfers between devices, local(): lax.psum_scatter(normed_two_part.astype(bf_type), 'tensor', scatter_dimen...  10.2 us
    unnamed x146, local copies, waits for them, and re-layouts  10 us
    slice x4, local copies, waits for them, and re-layouts, sum_near(): return (kept[2:], core[2:], first)  9.59 us
  transfers between devices with their start and end apart: 43, of which 23 were waited for; matrix products, arithmetic and copies ran while one was open for 21% of the time, Pallas kernels for 9%

profile of v1, /device:TPU:0, one launch (start us, length us, event | category | flops | bytes accessed | tf_op | source)
XLA Modules:
  0.0 382.0 jit_solution(11605690113275266368)
XLA Ops:
  8.9 3.0 collective-permute-start
  13.5 1.5 collective-permute-start.3
  15.0 2.0 shard_map.212
  18.6 1.8 fusion.29
  21.7 5.1 %collective-permute-done.1 = bf16[2,128,384]{2,1,0:T(8,128)(2,1)S(1)} collective-permute-done((bf16[2,128,384]{2,1,0:T(8,128)(2,1)S(1)}, bf16[2,128,384]{2,1,0:T(8,128)(2,1)S(1)}, u32[]{:S(2)}, u32[]{:S(2)}) %collective-permute-start.1) | collective-permute-done | bytes 196640 | tf_op jit(solution)/shard_map/ppermute | solution.py:72
  29.8 18.1 %all-gather.4.cloned.1.call-done = bf16[512,1024]{1,0:T(8,128)(2,1)} async-done(((bf16[128,1024]{1,0:T(8,128)(2,1)}), bf16[512,1024]{1,0:T(8,128)(2,1)}) %all-gather.4.cloned.1.call-update) | async-done | bytes 1048592 | tf_op jit(solution)/shard_map/all_gather | solution.py:341
  47.9 1.9 fusion.64
  52.4 1.4 copy-done.8
  54.6 1.5 convolution_convert_fusion
  56.3 1.5 collective-permute-start.9
  58.0 1.5 collective-permute-start.10
  59.5 16.0 %collective-permute-done.9 = bf16[3,8,128,128]{3,2,1,0:T(8,128)(2,1)S(1)} collective-permute-done((bf16[3,8,128,128]{3,2,1,0:T(8,128)(2,1)S(1)}, bf16[3,8,128,128]{3,2,1,0:T(8,128)(2,1)S(1)}, u32[]{:S(2)}, u32[]{:S(2)}) %collective-permute-start.9) | collective-permute-done | bytes 786464 | tf_op jit(solution)/shard_map/ppermute | solution.py:72
  75.7 1.5 collective-permute-start.11
  78.5 1.5 collective-permute-start.12
  80.0 2.9 reduce-scatter.4.cloned.1.call-done
  84.1 1.8 multiply_convert_fusion
  86.1 25.0 %collective-permute-done.11.second = bf16[2,3,8,128,128]{4,3,2,1,0:T(8,128)(2,1)} collective-permute-done((bf16[2,3,8,128,128]{4,3,2,1,0:T(8,128)(2,1)S(1)}, bf16[2,3,8,128,128]{4,3,2,1,0:T(8,128)(2,1)}, u32[]{:S(2)}, u32[]{:S(2)}) %collective-permute-start.11) | collective-permute-done | bytes 1572896 | tf_op jit(solution)/shard_map/ppermute | solution.py:72
  111.1 2.7 collective-permute-done.12.second
  114.3 2.6 collective-permute-start.8
  117.4 7.1 %collective-permute-done.8 = bf16[128,1024]{1,0:T(8,128)(2,1)S(1)} collective-permute-done((bf16[128,1024]{1,0:T(8,128)(2,1)S(1)}, bf16[128,1024]{1,0:T(8,128)(2,1)S(1)}, u32[]{:S(2)}, u32[]{:S(2)}) %collective-permute-start.8) | collective-permute-done | bytes 262176 | tf_op jit(solution)/shard_map/ppermute | solution.py:72
  124.4 5.9 %collective-permute-start.7 = (bf16[128,1024]{1,0:T(8,128)(2,1)S(1)}, bf16[128,1024]{1,0:T(8,128)(2,1)S(1)}, u32[]{:S(2)}, u32[]{:S(2)}) collective-permute-start(bf16[128,1024]{1,0:T(8,128)(2,1)S(1)} %copy-done.28), channel_id=1, source_target_pairs={{0,2},{1,3},{2,0},{3,1},{4,6},{5,7},{6,4},{7,5},{8,10},{9,11},{10,... | collective-permute-start | bytes 786440 | tf_op jit(solution)/shard_map/ppermute | solution.py:72
  130.3 11.2 %collective-permute-done.7 = bf16[128,1024]{1,0:T(8,128)(2,1)S(1)} collective-permute-done((bf16[128,1024]{1,0:T(8,128)(2,1)S(1)}, bf16[128,1024]{1,0:T(8,128)(2,1)S(1)}, u32[]{:S(2)}, u32[]{:S(2)}) %collective-permute-start.7) | collective-permute-done | bytes 262176 | tf_op jit(solution)/shard_map/ppermute | solution.py:72
  141.8 6.8 %collective-permute-done.6 = bf16[128,1024]{1,0:T(8,128)(2,1)S(1)} collective-permute-done((bf16[128,1024]{1,0:T(8,128)(2,1)S(1)}, bf16[128,1024]{1,0:T(8,128)(2,1)S(1)}, u32[]{:S(2)}, u32[]{:S(2)}) %collective-permute-start.6) | collective-permute-done | bytes 262176 | tf_op jit(solution)/shard_map/ppermute | solution.py:72
  149.8 16.3 %shard_map.213 = (f32[512,1024]{1,0:T(8,128)}, f32[512,1024]{1,0:T(8,128)}, bf16[512,1024]{1,0:T(8,128)(2,1)S(1)}, bf16[512,1024]{1,0:T(8,128)(2,1)S(1)}, bf16[512,1024]{1,0:T(8,128)(2,1)S(1)}) custom-call(bf16[512,1024]{1,0:T(8,128)(2,1)} %all-gather.6.cloned.1.call-done.x, bf16[512,1024]{1,0:T(8,128)(2,1)} %pad_maximum_fusion.3.dy, ...), custom_call_target="tpu_custom_call" | custom-call | flops 6442450944 | bytes 16777216 | tf_op jit(solution)/shard_map/pallas_call | solution.py:167
  167.1 16.6 %shard_map.214 = (f32[512,1024]{1,0:T(8,128)}, f32[512,1024]{1,0:T(8,128)}, bf16[512,1024]{1,0:T(8,128)(2,1)S(1)}, bf16[512,1024]{1,0:T(8,128)(2,1)S(1)}, bf16[512,1024]{1,0:T(8,128)(2,1)S(1)}) custom-call(bf16[512,1024]{1,0:T(8,128)(2,1)} %all-gather.6.cloned.1.call-done.x, bf16[512,1024]{1,0:T(8,128)(2,1)} %pad_maximum_fusion.3.dy, ...), custom_call_target="tpu_custom_call" | custom-call | flops 6442450944 | bytes 16777216 | tf_op jit(solution)/shard_map/pallas_call | solution.py:167
  186.6 3.0 add_convert_fusion.2
  189.7 7.1 %shard_map.215 = (bf16[4,3,8,128,128]{4,3,2,1,0:T(8,128)(2,1)}, bf16[4,3,8,128,128]{4,3,2,1,0:T(8,128)(2,1)}) custom-call(bf16[512,1024]{1,0:T(8,128)(2,1)S(1)} %copy-done.1, bf16[512,1024]{1,0:T(8,128)(2,1)S(1)} %copy-done, bf16[512,1024]{1,0:T(8,128)(2,1)S(1)} %get-tuple-element.114.hg, bf16[512,1024]{1,0:T(8,128)(2,1)} %copy-done.2, ...), custom_call_target="tpu_custom_call" | custom-call | flops 3221225472 | bytes 10485760 | tf_op jit(solution)/shard_map/pallas_call | solution.py:201
  196.9 7.2 %shard_map.216 = (bf16[4,3,8,128,128]{4,3,2,1,0:T(8,128)(2,1)}, bf16[4,3,8,128,128]{4,3,2,1,0:T(8,128)(2,1)}) custom-call(bf16[512,1024]{1,0:T(8,128)(2,1)S(1)} %copy-done.1, bf16[512,1024]{1,0:T(8,128)(2,1)S(1)} %copy-done, bf16[512,1024]{1,0:T(8,128)(2,1)S(1)} %copy-done.5, bf16[512,1024]{1,0:T(8,128)(2,1)} %copy-done.6, bf16[512,1024]{1,0:T(8,128)(2,1)} %copy-done.7), custom_call_target="tpu_custom_call" | custom-call | flops 3221225472 | bytes 10485760 | tf_op jit(solution)/shard_map/pallas_call | solution.py:201
  204.6 10.2 %reduce-scatter.6.cloned.1.call-done = bf16[128,1024]{1,0:T(8,128)(2,1)} async-done(((bf16[512,1024]{1,0:T(8,128)(2,1)}), bf16[128,1024]{1,0:T(8,128)(2,1)}) %reduce-scatter.6.cloned.1.call-update) | async-done | bytes 262160 | tf_op jit(solution)/shard_map/reduce_scatter | solution.py:425
  216.5 1.9 fusion.58
  219.6 2.8 slice.182
  224.6 2.1 add_convert_fusion.3
  227.2 3.7 add_convert_fusion.1
  231.0 1.5 collective-permute-start.21
  232.4 3.2 add_convert_fusion
  235.6 1.5 collective-permute-start.23
  237.1 2.7 slice.230
  239.8 2.8 slice.232
  242.6 2.6 all-gather.8.cloned.1.call-done
  245.2 1.7 convolution_convert_fusion.4
  247.8 1.4 collective-permute-start.17
  249.3 1.9 collective-permute-start.19
  251.3 3.3 fusion
  259.1 8.3 %collective-permute-done.21 = bf16[2,3,8,128,128]{4,3,2,1,0:T(8,128)(2,1)} collective-permute-done((bf16[2,3,8,128,128]{4,3,2,1,0:T(8,128)(2,1)}, bf16[2,3,8,128,128]{4,3,2,1,0:T(8,128)(2,1)}, u32[]{:S(2)}, u32[]{:S(2)}) %collective-permute-start.21) | collective-permute-done | bytes 1572896 | tf_op jit(solution)/shard_map/ppermute | solution.py:72
  267.3 4.4 %collective-permute-done.23 = bf16[2,3,8,128,128]{4,3,2,1,0:T(8,128)(2,1)} collective-permute-done((bf16[2,3,8,128,128]{4,3,2,1,0:T(8,128)(2,1)}, bf16[2,3,8,128,128]{4,3,2,1,0:T(8,128)(2,1)}, u32[]{:S(2)}, u32[]{:S(2)}) %collective-permute-start.23) | collective-permute-done | bytes 1572896 | tf_op jit(solution)/shard_map/ppermute | solution.py:72
  272.0 1.4 fusion.44
  276.0 1.9 copy.65
  279.9 3.0 multiply_reduce_fusion
  285.3 3.2 convert_add_fusion
  291.1 2.3 collective-permute-done.25
  293.4 1.5 collective-permute-start.26
  295.8 2.4 copy.64
  298.2 1.8 copy.52
  300.2 2.2 convert_add_fusion.1
  302.4 1.4 collective-permute-done.27
  305.2 3.9 %collective-permute-done.28 = f32[2,1024]{1,0:T(2,128)S(1)} collective-permute-done((f32[2,1024]{1,0:T(2,128)S(1)}, f32[2,1024]{1,0:T(2,128)S(1)}, u32[]{:S(2)}, u32[]{:S(2)}) %collective-permute-start.28) | collective-permute-done | bytes 8224 | tf_op jit(solution)/shard_map/ppermute | solution.py:72
  311.5 1.7 collective-permute-start.33
  313.4 20.5 %collective-permute-done.33 = bf16[2,128,384]{2,1,0:T(8,128)(2,1)S(1)} collective-permute-done((bf16[2,128,384]{2,1,0:T(8,128)(2,1)S(1)}, bf16[2,128,384]{2,1,0:T(8,128)(2,1)S(1)}, u32[]{:S(2)}, u32[]{:S(2)}) %collective-permute-start.33) | collective-permute-done | bytes 196640 | tf_op jit(solution)/shard_map/ppermute | solution.py:72
  334.4 6.1 %collective-permute-done.30 = bf16[2,128,384]{2,1,0:T(8,128)(2,1)S(1)} collective-permute-done((bf16[2,128,384]{2,1,0:T(8,128)(2,1)S(1)}, bf16[2,128,384]{2,1,0:T(8,128)(2,1)S(1)}, u32[]{:S(2)}, u32[]{:S(2)}) %collective-permute-start.30) | collective-permute-done | bytes 196640 | tf_op jit(solution)/shard_map/ppermute | solution.py:72
  340.9 4.1 %collective-permute-done.34 = bf16[128,384]{1,0:T(8,128)(2,1)S(1)} collective-permute-done((bf16[128,384]{1,0:T(8,128)(2,1)S(1)}, bf16[128,384]{1,0:T(8,128)(2,1)S(1)}, u32[]{:S(2)}, u32[]{:S(2)}) %collective-permute-start.34) | collective-permute-done | bytes 98336 | tf_op jit(solution)/shard_map/ppermute | solution.py:72
  346.8 2.9 collective-permute-done.31
  351.8 13.9 %collective-permute-done.36 = bf16[3,8,128,128]{3,2,1,0:T(8,128)(2,1)S(1)} collective-permute-done((bf16[3,8,128,128]{3,2,1,0:T(8,128)(2,1)S(1)}, bf16[3,8,128,128]{3,2,1,0:T(8,128)(2,1)S(1)}, u32[]{:S(2)}, u32[]{:S(2)}) %collective-permute-start.36) | collective-permute-done | bytes 786464 | tf_op jit(solution)/shard_map/ppermute | solution.py:72
  370.4 2.6 fusion.32
  373.0 2.2 shard_map.217
  (288 shorter events, 57.4 us)
Async XLA Ops:
  7.2 13.3 %copy-start.47 = (bf16[16,128,128]{2,1,0:T(8,128)(2,1)S(1)}, bf16[16,128,128]{2,1,0:T(8,128)(2,1)}, u32[]{:S(2)}) copy-start(bf16[16,128,128]{2,1,0:T(8,128)(2,1)} %param.20) | copy-start | bytes 1572868
  7.2 40.7 %all-gather.4.cloned.1.call-start = ((), (), s32[]{:S(2)}) async-start(), calls=%async_computation.3 | async-start | bytes 1310720 | tf_op jit(solution)/shard_map/all_gather | solution.py:341
  8.9 11.7 %collective-permute-start = (bf16[128,384]{1,0:T(8,128)(2,1)S(1)}, bf16[128,384]{1,0:T(8,128)(2,1)S(1)}, u32[]{:S(2)}, u32[]{:S(2)}) collective-permute-start(bf16[128,384]{1,0:T(8,128)(2,1)S(1)} %constant_dynamic-update-slice_fusion), channel_id=1, source_target_pairs={{0,16},{4,20},{8,24},{12,28},{16,0},{20,4},{24,8},{28,12},{1,17},{... | collective-permute-start | bytes 294920 | tf_op jit(solution)/shard_map/ppermute | solution.py:72
  13.5 8.1 %collective-permute-start.3 = (bf16[128,384]{1,0:T(8,128)(2,1)S(1)}, bf16[128,384]{1,0:T(8,128)(2,1)S(1)}, u32[]{:S(2)}, u32[]{:S(2)}) collective-permute-start(bf16[128,384]{1,0:T(8,128)(2,1)S(1)} %constant_dynamic-update-slice_fusion.2), channel_id=1, source_target_pairs={{0,8},{4,12},{8,0},{12,4},{16,24},{20,28},{24,16},{28,20},{1,9},{5... | collective-permute-start | bytes 294920 | tf_op jit(solution)/shard_map/ppermute | solution.py:72
  20.5 62.5 %reduce-scatter.4.cloned.1.call-start = ((), (), s32[]{:S(2)}) async-start(), calls=%async_computation.4 | async-start | bytes 1310720 | tf_op jit(solution)/shard_map/reduce_scatter | solution.py:389
  20.7 6.1 %collective-permute-start.1 = (bf16[2,128,384]{2,1,0:T(8,128)(2,1)S(1)}, bf16[2,128,384]{2,1,0:T(8,128)(2,1)S(1)}, u32[]{:S(2)}, u32[]{:S(2)}) collective-permute-start(bf16[2,128,384]{2,1,0:T(8,128)(2,1)S(1)} %get-tuple-element.180), channel_id=1, source_target_pairs={{0,8},{4,12},{8,0},{12,4},{16,24},{20,28},{24,16},{28,20},{1,9},{5... | collective-permute-start | bytes 589832 | tf_op jit(solution)/shard_map/ppermute | solution.py:72
  21.6 6.1 %collective-permute-start.4 = (bf16[2,128,384]{2,1,0:T(8,128)(2,1)S(1)}, bf16[2,128,384]{2,1,0:T(8,128)(2,1)S(1)}, u32[]{:S(2)}, u32[]{:S(2)}) collective-permute-start(bf16[2,128,384]{2,1,0:T(8,128)(2,1)S(1)} %get-tuple-element.178), channel_id=1, source_target_pairs={{0,16},{4,20},{8,24},{12,28},{16,0},{20,4},{24,8},{28,12},{1,17},{... | collective-permute-start | bytes 589832 | tf_op jit(solution)/shard_map/ppermute | solution.py:72
  26.9 1.8 collective-permute-start.2
  27.8 1.9 collective-permute-start.5
  28.7 25.9 %copy-start.20 = (bf16[4,2,128,384]{3,2,1,0:T(8,128)(2,1)}, bf16[4,2,128,384]{3,2,1,0:T(8,128)(2,1)S(1)}, u32[]{:S(2)}) copy-start(bf16[4,2,128,384]{3,2,1,0:T(8,128)(2,1)S(1)} %pad_maximum_fusion.7) | copy-start | bytes 2359300
  29.8 20.1 %copy-start.15 = (bf16[4,2,128,384]{3,2,1,0:T(8,128)(2,1)}, bf16[4,2,128,384]{3,2,1,0:T(8,128)(2,1)S(1)}, u32[]{:S(2)}) copy-start(bf16[4,2,128,384]{3,2,1,0:T(8,128)(2,1)S(1)} %pad_maximum_fusion.8) | copy-start | bytes 2359300
  56.1 93.7 %all-gather.6.cloned.1.call-start = ((), (), s32[]{:S(2)}) async-start(), calls=%async_computation.5 | async-start | bytes 1310720 | tf_op jit(solution)/shard_map/all_gather | solution.py:394
  56.3 19.2 %collective-permute-start.9 = (bf16[3,8,128,128]{3,2,1,0:T(8,128)(2,1)S(1)}, bf16[3,8,128,128]{3,2,1,0:T(8,128)(2,1)S(1)}, u32[]{:S(2)}, u32[]{:S(2)}) collective-permute-start(bf16[3,8,128,128]{3,2,1,0:T(8,128)(2,1)S(1)} %get-tuple-element.160), channel_id=1, source_target_pairs={{0,8},{4,12},{8,0},{12,4},{16,24},{20,28},{24,16},{28,20},{1,9},{5... | collective-permute-start | bytes 2359304 | tf_op jit(solution)/shard_map/ppermute | solution.py:72
  58.0 19.3 %collective-permute-start.10 = (bf16[3,8,128,128]{3,2,1,0:T(8,128)(2,1)S(1)}, bf16[3,8,128,128]{3,2,1,0:T(8,128)(2,1)S(1)}, u32[]{:S(2)}, u32[]{:S(2)}) collective-permute-start(bf16[3,8,128,128]{3,2,1,0:T(8,128)(2,1)S(1)} %get-tuple-element.158), channel_id=1, source_target_pairs={{0,16},{4,20},{8,24},{12,28},{16,0},{20,4},{24,8},{28,12},{1,17},{... | collective-permute-start | bytes 2359304 | tf_op jit(solution)/shard_map/ppermute | solution.py:72
  75.7 38.1 %copy-start.33 = (bf16[2,3,8,128,128]{4,3,2,1,0:T(8,128)(2,1)}, bf16[2,3,8,128,128]{4,3,2,1,0:T(8,128)(2,1)S(1)}, u32[]{:S(2)}) copy-start(bf16[2,3,8,128,128]{4,3,2,1,0:T(8,128)(2,1)S(1)} %pad_maximum_fusion.pair) | copy-start | bytes 4718596
  75.7 8.4 %copy-start.56 = (f32[1,1024]{1,0:T(1,128)S(1)}, f32[1,1024]{1,0:T(1,128)}, u32[]{:S(2)}) copy-start(f32[1,1024]{1,0:T(1,128)} %get-tuple-element.103) | copy-start | bytes 12292
  75.7 35.4 %collective-permute-start.11 = (bf16[2,3,8,128,128]{4,3,2,1,0:T(8,128)(2,1)S(1)}, bf16[2,3,8,128,128]{4,3,2,1,0:T(8,128)(2,1)}, u32[]{:S(2)}, u32[]{:S(2)}) collective-permute-start(bf16[2,3,8,128,128]{4,3,2,1,0:T(8,128)(2,1)S(1)} %pad_maximum_fusion.pair), channel_id=1, source_target_pairs={{0,16},{4,20},{8,24},{12,28},{16,0},{20,4},{24,8},{28,12},{1,17},{... | collective-permute-start | bytes 4718600 | tf_op jit(solution)/shard_map/ppermute | solution.py:72
  77.2 37.1 %copy-start.28 = (bf16[128,1024]{1,0:T(8,128)(2,1)S(1)}, bf16[128,1024]{1,0:T(8,128)(2,1)}, u32[]{:S(2)}) copy-start(bf16[128,1024]{1,0:T(8,128)(2,1)} %get-tuple-element.104) | copy-start | bytes 786436
  77.2 64.3 %copy-start.61 = (f32[512,8]{0,1:T(8,128)S(1)}, f32[512,8]{0,1:T(8,128)}, u32[]{:S(2)}) copy-start(f32[512,8]{0,1:T(8,128)} %param.24) | copy-start | bytes 49156
  77.2 64.3 %copy-start.62 = (s32[512,8]{0,1:T(8,128)S(1)}, s32[512,8]{0,1:T(8,128)}, u32[]{:S(2)}) copy-start(s32[512,8]{0,1:T(8,128)} %param.23) | copy-start | bytes 49156
  78.5 35.2 %collective-permute-start.12 = (bf16[2,3,8,128,128]{4,3,2,1,0:T(8,128)(2,1)}, bf16[2,3,8,128,128]{4,3,2,1,0:T(8,128)(2,1)}, u32[]{:S(2)}, u32[]{:S(2)}) collective-permute-start(bf16[2,3,8,128,128]{4,3,2,1,0:T(8,128)(2,1)} %pad_maximum_fusion.1.pair), channel_id=1, source_target_pairs={{0,8},{4,12},{8,0},{12,4},{16,24},{20,28},{24,16},{28,20},{1,9},{5... | collective-permute-start | bytes 4718600 | tf_op jit(solution)/shard_map/ppermute | solution.py:72
  84.1 131.9 %copy-start.63 = (f32[128]{0:T(128)}, f32[128]{0:T(128)S(1)}, u32[]{:S(2)}) copy-start(f32[128]{0:T(128)S(1)} %get-tuple-element.186) | copy-start | bytes 1540
  84.1 131.9 %copy-start.67 = (f32[128]{0:T(128)}, f32[128]{0:T(128)S(1)}, u32[]{:S(2)}) copy-start(f32[128]{0:T(128)S(1)} %get-tuple-element.185) | copy-start | bytes 1540
  85.9 128.9 %reduce-scatter.6.cloned.1.call-start = ((), (), s32[]{:S(2)}) async-start(), calls=%async_computation.6 | async-start | bytes 1310720 | tf_op jit(solution)/shard_map/reduce_scatter | solution.py:425
  113.8 36.0 %collective-permute-start.13 = (bf16[2,3,8,128,128]{4,3,2,1,0:T(8,128)(2,1)S(1)}, bf16[2,3,8,128,128]{4,3,2,1,0:T(8,128)(2,1)}, u32[]{:S(2)}, u32[]{:S(2)}) collective-permute-start(bf16[2,3,8,128,128]{4,3,2,1,0:T(8,128)(2,1)S(1)} %pad_maximum_fusion.pair), channel_id=1, source_target_pairs={{0,4},{4,0},{8,12},{12,8},{16,20},{20,16},{24,28},{28,24},{1,5},{5... | collective-permute-start | bytes 4718600 | tf_op jit(solution)/shard_map/ppermute | solution.py:72
  113.8 36.0 %collective-permute-start.14 = (bf16[2,3,8,128,128]{4,3,2,1,0:T(8,128)(2,1)}, bf16[2,3,8,128,128]{4,3,2,1,0:T(8,128)(2,1)}, u32[]{:S(2)}, u32[]{:S(2)}) collective-permute-start(bf16[2,3,8,128,128]{4,3,2,1,0:T(8,128)(2,1)} %collective-permute-done.11.second), channel_id=1, source_target_pairs={{0,4},{4,0},{8,12},{12,8},{16,20},{20,16},{24,28},{28,24},{1,5},{5... | collective-permute-start | bytes 4718600 | tf_op jit(solution)/shard_map/ppermute | solution.py:72
  114.3 10.1 %collective-permute-start.8 = (bf16[128,1024]{1,0:T(8,128)(2,1)S(1)}, bf16[128,1024]{1,0:T(8,128)(2,1)S(1)}, u32[]{:S(2)}, u32[]{:S(2)}) collective-permute-start(bf16[128,1024]{1,0:T(8,128)(2,1)S(1)} %copy-done.28), channel_id=1, source_target_pairs={{0,3},{1,2},{2,1},{3,0},{4,7},{5,6},{6,5},{7,4},{8,11},{9,10},{10,... | collective-permute-start | bytes 786440 | tf_op jit(solution)/shard_map/ppermute | solution.py:72
  116.9 50.2 %collective-permute-start.15 = (bf16[2,3,8,128,128]{4,3,2,1,0:T(8,128)(2,1)}, bf16[2,3,8,128,128]{4,3,2,1,0:T(8,128)(2,1)}, u32[]{:S(2)}, u32[]{:S(2)}) collective-permute-start(bf16[2,3,8,128,128]{4,3,2,1,0:T(8,128)(2,1)} %pad_maximum_fusion.1.pair), channel_id=1, source_target_pairs={{0,4},{4,0},{8,12},{12,8},{16,20},{20,16},{24,28},{28,24},{1,5},{5... | collective-permute-start | bytes 4718600 | tf_op jit(solution)/shard_map/ppermute | solution.py:72
  116.9 50.2 %collective-permute-start.16 = (bf16[2,3,8,128,128]{4,3,2,1,0:T(8,128)(2,1)}, bf16[2,3,8,128,128]{4,3,2,1,0:T(8,128)(2,1)}, u32[]{:S(2)}, u32[]{:S(2)}) collective-permute-start(bf16[2,3,8,128,128]{4,3,2,1,0:T(8,128)(2,1)} %collective-permute-done.12.second), channel_id=1, source_target_pairs={{0,4},{4,0},{8,12},{12,8},{16,20},{20,16},{24,28},{28,24},{1,5},{5... | collective-permute-start | bytes 4718600 | tf_op jit(solution)/shard_map/ppermute | solution.py:72
  124.4 17.1 %collective-permute-start.7 = (bf16[128,1024]{1,0:T(8,128)(2,1)S(1)}, bf16[128,1024]{1,0:T(8,128)(2,1)S(1)}, u32[]{:S(2)}, u32[]{:S(2)}) collective-permute-start(bf16[128,1024]{1,0:T(8,128)(2,1)S(1)} %copy-done.28), channel_id=1, source_target_pairs={{0,2},{1,3},{2,0},{3,1},{4,6},{5,7},{6,4},{7,5},{8,10},{9,11},{10,... | collective-permute-start | bytes 786440 | tf_op jit(solution)/shard_map/ppermute | solution.py:72
  141.6 7.0 %collective-permute-start.6 = (bf16[128,1024]{1,0:T(8,128)(2,1)S(1)}, bf16[128,1024]{1,0:T(8,128)(2,1)S(1)}, u32[]{:S(2)}, u32[]{:S(2)}) collective-permute-start(bf16[128,1024]{1,0:T(8,128)(2,1)S(1)} %copy-done.28), channel_id=1, source_target_pairs={{0,1},{1,0},{2,3},{3,2},{4,5},{5,4},{6,7},{7,6},{8,9},{9,8},{10,11... | collective-permute-start | bytes 786440 | tf_op jit(solution)/shard_map/ppermute | solution.py:72
  167.1 16.6 %copy-start.2 = (bf16[512,1024]{1,0:T(8,128)(2,1)}, bf16[512,1024]{1,0:T(8,128)(2,1)S(1)}, u32[]{:S(2)}) copy-start(bf16[512,1024]{1,0:T(8,128)(2,1)S(1)} %get-tuple-element.115.gg) | copy-start | bytes 3145732
  167.1 19.5 %copy-start.32 = (f32[512,1024]{1,0:T(8,128)S(1)}, f32[512,1024]{1,0:T(8,128)}, u32[]{:S(2)}) copy-start(f32[512,1024]{1,0:T(8,128)} %get-tuple-element.111) | copy-start | bytes 6291460
  189.6 55.5 %all-gather.8.cloned.1.call-start = ((), (), s32[]{:S(2)}) async-start(), calls=%async_computation.7 | async-start | bytes 1310720 | tf_op jit(solution)/shard_map/all_gather | solution.py:444
  196.9 29.9 %collective-permute-start.20 = (bf16[4,3,8,128,128]{4,3,2,1,0:T(8,128)(2,1)}, bf16[4,3,8,128,128]{4,3,2,1,0:T(8,128)(2,1)}, u32[]{:S(2)}, u32[]{:S(2)}) collective-permute-start(bf16[4,3,8,128,128]{4,3,2,1,0:T(8,128)(2,1)} %get-tuple-element.118), channel_id=1, source_target_pairs={{0,4},{4,0},{8,12},{12,8},{16,20},{20,16},{24,28},{28,24},{1,5},{5... | collective-permute-start | bytes 9437192 | tf_op jit(solution)/shard_map/ppermute | solution.py:72
  196.9 17.9 %copy-start.16 = (bf16[128,1024]{1,0:T(8,128)(2,1)S(1)}, bf16[128,1024]{1,0:T(8,128)(2,1)}, u32[]{:S(2)}) copy-start(bf16[128,1024]{1,0:T(8,128)(2,1)} %reduce-scatter.4.cloned.1.call-done) | copy-start | bytes 786436
  196.9 19.6 %copy-start.29 = (bf16[128,1024]{1,0:T(8,128)(2,1)S(1)}, bf16[128,1024]{1,0:T(8,128)(2,1)}, u32[]{:S(2)}) copy-start(bf16[128,1024]{1,0:T(8,128)(2,1)} %get-tuple-element.104) | copy-start | bytes 786436
  204.1 28.4 %collective-permute-start.22 = (bf16[4,3,8,128,128]{4,3,2,1,0:T(8,128)(2,1)}, bf16[4,3,8,128,128]{4,3,2,1,0:T(8,128)(2,1)}, u32[]{:S(2)}, u32[]{:S(2)}) collective-permute-start(bf16[4,3,8,128,128]{4,3,2,1,0:T(8,128)(2,1)} %get-tuple-element.123), channel_id=1, source_target_pairs={{0,4},{4,0},{8,12},{12,8},{16,20},{20,16},{24,28},{28,24},{1,5},{5... | collective-permute-start | bytes 9437192 | tf_op jit(solution)/shard_map/ppermute | solution.py:72
  218.5 150.7 %reduce-scatter.8.cloned.1.call-start = ((), (), s32[]{:S(2)}) async-start(), calls=%async_computation.8 | async-start | bytes 1310720 | tf_op jit(solution)/shard_map/reduce_scatter | solution.py:509
  226.7 20.2 %copy-start.22 = (bf16[512,1024]{1,0:T(8,128)(2,1)}, bf16[512,1024]{1,0:T(8,128)(2,1)S(1)}, u32[]{:S(2)}) copy-start(bf16[512,1024]{1,0:T(8,128)(2,1)S(1)} %add_convert_fusion.3) | copy-start | bytes 3145732
  231.0 36.4 %collective-permute-start.21 = (bf16[2,3,8,128,128]{4,3,2,1,0:T(8,128)(2,1)}, bf16[2,3,8,128,128]{4,3,2,1,0:T(8,128)(2,1)}, u32[]{:S(2)}, u32[]{:S(2)}) collective-permute-start(bf16[2,3,8,128,128]{4,3,2,1,0:T(8,128)(2,1)} %add_convert_fusion.1), channel_id=1, source_target_pairs={{0,8},{4,12},{8,0},{12,4},{16,24},{20,28},{24,16},{28,20},{1,9},{5... | collective-permute-start | bytes 4718600 | tf_op jit(solution)/shard_map/ppermute | solution.py:72
  235.6 36.1 %collective-permute-start.23 = (bf16[2,3,8,128,128]{4,3,2,1,0:T(8,128)(2,1)}, bf16[2,3,8,128,128]{4,3,2,1,0:T(8,128)(2,1)}, u32[]{:S(2)}, u32[]{:S(2)}) collective-permute-start(bf16[2,3,8,128,128]{4,3,2,1,0:T(8,128)(2,1)} %add_convert_fusion), channel_id=1, source_target_pairs={{0,16},{4,20},{8,24},{12,28},{16,0},{20,4},{24,8},{28,12},{1,17},{... | collective-permute-start | bytes 4718600 | tf_op jit(solution)/shard_map/ppermute | solution.py:72
  242.6 8.7 %copy-start.42 = (bf16[512,128]{0,1:T(8,128)(2,1)S(1)}, bf16[512,128]{0,1:T(8,128)(2,1)}, u32[]{:S(2)}) copy-start(bf16[512,128]{0,1:T(8,128)(2,1)} %copy-done.41) | copy-start | bytes 393220
  247.8 122.5 %collective-permute-start.17 = (bf16[128,1024]{1,0:T(8,128)(2,1)}, bf16[128,1024]{1,0:T(8,128)(2,1)}, u32[]{:S(2)}, u32[]{:S(2)}) collective-permute-start(bf16[128,1024]{1,0:T(8,128)(2,1)} %get-tuple-element.146), channel_id=1, source_target_pairs={{0,1},{1,0},{2,3},{3,2},{4,5},{5,4},{6,7},{7,6},{8,9},{9,8},{10,11... | collective-permute-start | bytes 786440 | tf_op jit(solution)/shard_map/ppermute | solution.py:72
  249.3 121.1 %collective-permute-start.19 = (bf16[128,1024]{1,0:T(8,128)(2,1)}, bf16[128,1024]{1,0:T(8,128)(2,1)}, u32[]{:S(2)}, u32[]{:S(2)}) collective-permute-start(bf16[128,1024]{1,0:T(8,128)(2,1)} %get-tuple-element.147), channel_id=1, source_target_pairs={{0,3},{1,2},{2,1},{3,0},{4,7},{5,6},{6,5},{7,4},{8,11},{9,10},{10,... | collective-permute-start | bytes 786440 | tf_op jit(solution)/shard_map/ppermute | solution.py:72
  251.2 119.2 %collective-permute-start.18 = (bf16[128,1024]{1,0:T(8,128)(2,1)}, bf16[128,1024]{1,0:T(8,128)(2,1)}, u32[]{:S(2)}, u32[]{:S(2)}) collective-permute-start(bf16[128,1024]{1,0:T(8,128)(2,1)} %get-tuple-element.148), channel_id=1, source_target_pairs={{0,2},{1,3},{2,0},{3,1},{4,6},{5,7},{6,4},{7,5},{8,10},{9,11},{10,... | collective-permute-start | bytes 786440 | tf_op jit(solution)/shard_map/ppermute | solution.py:72
  258.3 13.4 %copy-start.11 = (bf16[512,1024]{1,0:T(8,128)(2,1)S(1)}, bf16[512,1024]{1,0:T(8,128)(2,1)}, u32[]{:S(2)}) copy-start(bf16[512,1024]{1,0:T(8,128)(2,1)} %all-gather.4.cloned.1.call-done) | copy-start | bytes 3145732
  278.0 31.8 %collective-permute-start.32 = (bf16[2,2,128,384]{3,2,1,0:T(8,128)(2,1)}, bf16[2,2,128,384]{3,2,1,0:T(8,128)(2,1)}, u32[]{:S(2)}, u32[]{:S(2)}) collective-permute-start(bf16[2,2,128,384]{3,2,1,0:T(8,128)(2,1)} %bitcast.234), channel_id=1, source_target_pairs={{0,4},{4,0},{8,12},{12,8},{16,20},{20,16},{24,28},{28,24},{1,5},{5... | collective-permute-start | bytes 1179656 | tf_op jit(solution)/shard_map/ppermute | solution.py:72
  284.8 4.8 %collective-permute-start.24 = (f32[2,1024]{1,0:T(2,128)}, f32[2,1024]{1,0:T(2,128)S(1)}, u32[]{:S(2)}, u32[]{:S(2)}) collective-permute-start(f32[2,1024]{1,0:T(2,128)} %shard_map.218), channel_id=1, source_target_pairs={{0,4},{4,0},{8,12},{12,8},{16,20},{20,16},{24,28},{28,24},{1,5},{5... | collective-permute-start | bytes 24584 | tf_op jit(solution)/shard_map/ppermute | solution.py:72
  289.7 3.7 collective-permute-start.25
  293.4 6.7 %collective-permute-start.26 = (f32[2,1024]{1,0:T(2,128)S(1)}, f32[2,1024]{1,0:T(2,128)S(1)}, u32[]{:S(2)}, u32[]{:S(2)}) collective-permute-start(f32[2,1024]{1,0:T(2,128)S(1)} %add.182), channel_id=1, source_target_pairs={{0,16},{4,20},{8,24},{12,28},{16,0},{20,4},{24,8},{28,12},{1,17},{... | collective-permute-start | bytes 24584 | tf_op jit(solution)/shard_map/ppermute | solution.py:72
  300.1 9.0 %copy-start.50 = (bf16[2,2,128,384]{3,2,0,1:T(8,128)(2,1)S(1)}, bf16[2,2,128,384]{3,2,0,1:T(8,128)(2,1)}, u32[]{:S(2)}) copy-start(bf16[2,2,128,384]{3,2,0,1:T(8,128)(2,1)} %copy.52) | copy-start | bytes 1179652
  300.1 3.7 collective-permute-start.27
  302.4 10.8 %copy-start.34 = (bf16[512,384]{1,0:T(8,128)(2,1)S(1)}, bf16[512,384]{1,0:T(8,128)(2,1)}, u32[]{:S(2)}) copy-start(bf16[512,384]{1,0:T(8,128)(2,1)} %get-tuple-element.156) | copy-start | bytes 1179652
  303.8 5.3 %collective-permute-start.28 = (f32[2,1024]{1,0:T(2,128)S(1)}, f32[2,1024]{1,0:T(2,128)S(1)}, u32[]{:S(2)}, u32[]{:S(2)}) collective-permute-start(f32[2,1024]{1,0:T(2,128)S(1)} %add.184), channel_id=1, source_target_pairs={{0,2},{1,3},{2,0},{3,1},{4,6},{5,7},{6,4},{7,5},{8,10},{9,11},{10,... | collective-permute-start | bytes 24584 | tf_op jit(solution)/shard_map/ppermute | solution.py:72
  309.1 2.4 collective-permute-start.29
  309.7 41.7 %collective-permute-start.35 = (bf16[3,8,128,128]{3,2,1,0:T(8,128)(2,1)S(1)}, bf16[3,8,128,128]{3,2,1,0:T(8,128)(2,1)S(1)}, u32[]{:S(2)}, u32[]{:S(2)}) collective-permute-start(bf16[3,8,128,128]{3,2,1,0:T(8,128)(2,1)S(1)} %fusion.17), channel_id=1, source_target_pairs={{0,16},{4,20},{8,24},{12,28},{16,0},{20,4},{24,8},{28,12},{1,17},{... | collective-permute-start | bytes 2359304 | tf_op jit(solution)/shard_map/ppermute | solution.py:72
  311.2 38.4 %copy-start.40 = (bf16[3,8,128,128]{3,2,1,0:T(8,128)(2,1)S(1)}, bf16[3,8,128,128]{3,2,1,0:T(8,128)(2,1)}, u32[]{:S(2)}) copy-start(bf16[3,8,128,128]{3,2,1,0:T(8,128)(2,1)} %fusion.18) | copy-start | bytes 2359300
  311.5 22.4 %collective-permute-start.33 = (bf16[2,128,384]{2,1,0:T(8,128)(2,1)S(1)}, bf16[2,128,384]{2,1,0:T(8,128)(2,1)S(1)}, u32[]{:S(2)}, u32[]{:S(2)}) collective-permute-start(bf16[2,128,384]{2,1,0:T(8,128)(2,1)S(1)} %slice_bitcast_fusion.14), channel_id=1, source_target_pairs={{0,16},{4,20},{8,24},{12,28},{16,0},{20,4},{24,8},{28,12},{1,17},{... | collective-permute-start | bytes 589832 | tf_op jit(solution)/shard_map/ppermute | solution.py:72
  333.9 6.5 %collective-permute-start.30 = (bf16[2,128,384]{2,1,0:T(8,128)(2,1)S(1)}, bf16[2,128,384]{2,1,0:T(8,128)(2,1)S(1)}, u32[]{:S(2)}, u32[]{:S(2)}) collective-permute-start(bf16[2,128,384]{2,1,0:T(8,128)(2,1)S(1)} %slice_bitcast_fusion.16), channel_id=1, source_target_pairs={{0,8},{4,12},{8,0},{12,4},{16,24},{20,28},{24,16},{28,20},{1,9},{5... | collective-permute-start | bytes 589832 | tf_op jit(solution)/shard_map/ppermute | solution.py:72
  340.4 4.6 %collective-permute-start.34 = (bf16[128,384]{1,0:T(8,128)(2,1)S(1)}, bf16[128,384]{1,0:T(8,128)(2,1)S(1)}, u32[]{:S(2)}, u32[]{:S(2)}) collective-permute-start(bf16[128,384]{1,0:T(8,128)(2,1)S(1)} %slice_bitcast_fusion.18), channel_id=1, source_target_pairs={{0,8},{4,12},{8,0},{12,4},{16,24},{20,28},{24,16},{28,20},{1,9},{5... | collective-permute-start | bytes 294920 | tf_op jit(solution)/shard_map/ppermute | solution.py:72
  345.0 4.6 %collective-permute-start.31 = (bf16[128,384]{1,0:T(8,128)(2,1)S(1)}, bf16[128,384]{1,0:T(8,128)(2,1)S(1)}, u32[]{:S(2)}, u32[]{:S(2)}) collective-permute-start(bf16[128,384]{1,0:T(8,128)(2,1)S(1)} %slice_bitcast_fusion.20), channel_id=1, source_target_pairs={{0,16},{4,20},{8,24},{12,28},{16,0},{20,4},{24,8},{28,12},{1,17},{... | collective-permute-start | bytes 294920 | tf_op jit(solution)/shard_map/ppermute | solution.py:72
  349.7 16.0 %collective-permute-start.36 = (bf16[3,8,128,128]{3,2,1,0:T(8,128)(2,1)S(1)}, bf16[3,8,128,128]{3,2,1,0:T(8,128)(2,1)S(1)}, u32[]{:S(2)}, u32[]{:S(2)}) collective-permute-start(bf16[3,8,128,128]{3,2,1,0:T(8,128)(2,1)S(1)} %copy-done.40), channel_id=1, source_target_pairs={{0,8},{4,12},{8,0},{12,4},{16,24},{20,28},{24,16},{28,20},{1,9},{5... | collective-permute-start | bytes 2359304 | tf_op jit(solution)/shard_map/ppermute | solution.py:72
  351.6 14.0 %copy-start.14 = (f32[2,3,8,128,128]{4,3,2,1,0:T(8,128)S(1)}, f32[2,3,8,128,128]{4,3,2,1,0:T(8,128)}, u32[]{:S(2)}) copy-start(f32[2,3,8,128,128]{4,3,2,1,0:T(8,128)} %copy-done.13) | copy-start | bytes 9437188
  (51 other events, 154.0 us)
Sparse Core Ops, SparseCore 0:
  20.6 27.2 all-gather.3
  56.2 26.6 reduce-scatter.3
  86.0 26.5 all-gather.5
  189.8 24.9 reduce-scatter.5
  218.6 26.5 all-gather.7
  300.2 24.2 reduce-scatter.7
